TPU v7x, 128 devices: a whole 4x4x4 slice. The times are simulated.
128 devices in a mesh: tm: 16 (over x, z), rows: 8 (over y, core).
Axes of the slice: x: 4, y: 4, z: 4, core: 2. Of those that a mesh axis runs over, the one named last changes fastest.
Arguments:
- tile_values: bfloat16 [65536, 128, 128], P(('tm', 'rows')), may hold values from -6 to 6
- tile_users: int32 [65536], P(('tm', 'rows')), may hold values from 0 to 127
- tile_items: int32 [65536], P(('tm', 'rows')), may hold values from 0 to 127
- tile_steps: int32 [65536], P(('tm', 'rows')), may hold values from 0 to 7
- tile_count: int32 [128], P(('tm', 'rows')), may hold values from 64 to 512, as said below
- users_ask: int32 [16384, 1], P(('tm', 'rows')), may hold values from 0 to 7, as said below
- items_ask: int32 [16384, 1], P(('tm', 'rows')), may hold values from 0 to 7, as said below
- user_factor: float32 [1024, 64, 128], P(('tm', 'rows')), may hold values from -6 to 6
- item_factor: float32 [1024, 64, 128], P(('tm', 'rows')), may hold values from -6 to 6
- time_factor: float32 [128, 64], P('tm'), may hold values from -2 to 2
- core: float32 [64, 64, 64], replicated, may hold values from -0.25 to 0.25
Outputs:
- grad_users: float32 [1024, 64, 128], P(('tm', 'rows'))
- grad_items: float32 [1024, 64, 128], P(('tm', 'rows'))
- grad_time: float32 [128, 64], P('tm')
- grad_core: float32 [64, 64, 64], replicated
Inputs may be any that keep to these rules, and one draw needn't show every extreme that they name: `users_ask`: each row holds 1 distinct local block numbers of the owner that the row names. `items_ask`: each row holds 1 distinct local block numbers of the owner that the row names. `tile_count`: slots of a device at or past its count are padding; some device is full.
All inputs are finite; a program needn't handle non-finite values.
Results may differ from a plain program's by a relative error of at most 0.0003.
Values sent between devices are 32-bit elements; how exact they have to be, the bound alone decides.
No kernel may reach another device: no remote copies, remote signals or barrier semaphores. Data moves between devices by JAX's collectives and lax.ppermute only.
A program may use at most 128 MiB of HBM per device.

v0:
```python
import jax
import jax.numpy as jnp
from jax import lax
from jax.sharding import PartitionSpec as P

HIGH = lax.Precision.HIGHEST
user_scale = 0.125
time_scale = 1.0 / 2048.0
core_scale = 1.0 / 4096.0


def shards(
    tile_values,
    tile_users,
    tile_items,
    tile_steps,
    tile_count,
    users_ask,
    items_ask,
    user_factor,
    item_factor,
    time_factor,
    core,
):
    count_tm = lax.axis_size("tm")
    count_rows = lax.axis_size("rows")
    owners = count_tm * count_rows
    slot_cap = users_ask.shape[1]
    rank = user_factor.shape[1]
    width = user_factor.shape[2]
    blocks_own = user_factor.shape[0]
    step_count = time_factor.shape[0]
    tile_slots = tile_values.shape[0]
    ask_user = lax.all_to_all(users_ask, ("tm", "rows"), split_axis=0, concat_axis=0, tiled=True)
    ask_item = lax.all_to_all(items_ask, ("tm", "rows"), split_axis=0, concat_axis=0, tiled=True)
    found_user = jnp.take(user_factor, ask_user, axis=0)
    found_item = jnp.take(item_factor, ask_item, axis=0)
    back_user = lax.all_to_all(found_user, ("tm", "rows"), split_axis=0, concat_axis=0, tiled=True)
    back_item = lax.all_to_all(found_item, ("tm", "rows"), split_axis=0, concat_axis=0, tiled=True)
    fetched_user = back_user
    fetched_item = back_item
    held_user = ask_user
    held_item = ask_item
    fetched_user = fetched_user.reshape(owners * slot_cap, rank, width)
    fetched_item = fetched_item.reshape(owners * slot_cap, rank, width)
    held_user = held_user.reshape(owners * slot_cap)
    held_item = held_item.reshape(owners * slot_cap)
    step_cores = jnp.einsum("pqr,sr->spq", core, time_factor, precision=HIGH)
    block_size = min(64, tile_slots)
    live_count = tile_count[0]
    block_total = (live_count + block_size - 1) // block_size
    step_ids = jnp.arange(step_count, dtype=jnp.int32)

    def one_block(index, carry):
        grad_left, grad_right, step_sums = carry
        start = index * block_size
        values = lax.dynamic_slice_in_dim(tile_values, start, block_size, 0).astype(jnp.float32)
        slots_user = lax.dynamic_slice_in_dim(tile_users, start, block_size, 0)
        slots_item = lax.dynamic_slice_in_dim(tile_items, start, block_size, 0)
        local_steps = lax.dynamic_slice_in_dim(tile_steps, start, block_size, 0)
        picker = (local_steps[:, None] == step_ids[None, :]).astype(jnp.float32)
        cores = jnp.einsum("ts,spq->tpq", picker, step_cores, precision=HIGH)
        left = jnp.take(fetched_user, slots_user, axis=0)
        right = jnp.take(fetched_item, slots_item, axis=0)
        live = (start + jnp.arange(block_size, dtype=jnp.int32) < live_count).astype(jnp.float32)
        mixed = jnp.einsum("tpq,tqj->tpj", cores, right, precision=HIGH)
        guess = jnp.einsum("tpi,tpj->tij", left, mixed, precision=HIGH)
        resid = (guess - values) * live[:, None, None]
        grad_u = jnp.einsum("tij,tpj->tpi", resid, mixed, precision=HIGH)
        across = jnp.einsum("tpi,tpq->tqi", left, cores, precision=HIGH)
        grad_v = jnp.einsum("tij,tqi->tqj", resid, across, precision=HIGH)
        inner = jnp.einsum("tpi,tij->tpj", left, resid, precision=HIGH)
        dcore = jnp.einsum("tpj,tqj->tpq", inner, right, precision=HIGH)
        grad_left = grad_left.at[slots_user].add(grad_u)
        grad_right = grad_right.at[slots_item].add(grad_v)
        step_sums = step_sums + jnp.einsum("ts,tpq->spq", picker, dcore, precision=HIGH)
        return (grad_left, grad_right, step_sums)

    start_carry = (
        jnp.zeros((owners * slot_cap, rank, width), jnp.float32),
        jnp.zeros((owners * slot_cap, rank, width), jnp.float32),
        jnp.zeros((step_count, rank, rank), jnp.float32),
    )
    slot_left, slot_right, step_sums = lax.fori_loop(0, block_total, one_block, start_carry)
    back_left, back_right = (
        lax.all_to_all(
            slot_left.reshape(owners, slot_cap, rank, width),
            ("tm", "rows"),
            split_axis=0,
            concat_axis=0,
            tiled=True,
        ),
        lax.all_to_all(
            slot_right.reshape(owners, slot_cap, rank, width),
            ("tm", "rows"),
            split_axis=0,
            concat_axis=0,
            tiled=True,
        ),
    )
    own_ids = jnp.arange(blocks_own, dtype=jnp.int32)
    owner_user = (held_user[:, None] == own_ids[None, :]).astype(jnp.float32)
    owner_item = (held_item[:, None] == own_ids[None, :]).astype(jnp.float32)
    grad_users = user_scale * jnp.einsum(
        "nb,npi->bpi", owner_user, back_left.reshape(owners * slot_cap, rank, width), precision=HIGH
    )
    grad_items = user_scale * jnp.einsum(
        "nb,npi->bpi",
        owner_item,
        back_right.reshape(owners * slot_cap, rank, width),
        precision=HIGH,
    )
    slice_total = lax.psum(step_sums, "rows")
    grad_time = time_scale * jnp.einsum("spq,pqr->sr", slice_total, core, precision=HIGH)
    own_term = jnp.einsum("spq,sr->pqr", step_sums, time_factor, precision=HIGH)
    core_total = lax.psum(own_term, ("tm", "rows"))
    grad_core = core_scale * core_total
    return (grad_users, grad_items, grad_time, grad_core)


def solution(mesh):
    in_specs = (
        P(("tm", "rows"), None, None),
        P(("tm", "rows")),
        P(("tm", "rows")),
        P(("tm", "rows")),
        P(("tm", "rows")),
        P(("tm", "rows"), None),
        P(("tm", "rows"), None),
        P(("tm", "rows"), None, None),
        P(("tm", "rows"), None, None),
        P("tm", None),
        P(),
    )
    out_specs = (P(("tm", "rows"), None, None), P(("tm", "rows"), None, None), P("tm", None), P())
    return jax.shard_map(shards, mesh=mesh, in_specs=in_specs, out_specs=out_specs, check_vma=False)
```

profile of v0, /device:TPU:1, one launch (start us, length us, event | category | flops | bytes accessed | tf_op | source)
XLA Modules:
  0.0 1153.7 jit_solution(9990817299367265279)
XLA Ops:
  8.7 11.5 all-to-all-start.1
  21.6 8.0 all-to-all-done.1
  44.0 10.2 all-to-all-start.2
  63.9 42.8 %all-to-all-done.2 = f32[128,1,64,128]{3,2,1,0:T(8,128)} async-done(((f32[128,1,64,128]{3,2,1,0:T(8,128)}), f32[128,1,64,128]{3,2,1,0:T(8,128)}, u32[]{:S(2)}, u32[]{:S(2)}) %all-to-all-start.2) | async-done | bytes 4194336 | tf_op jit(solution)/shard_map/all_to_all | solution.py:39
  106.8 6.0 all-to-all-start.3
  118.5 46.9 %all-to-all-done.3 = f32[128,1,64,128]{3,2,1,0:T(8,128)} async-done(((f32[128,1,64,128]{3,2,1,0:T(8,128)}), f32[128,1,64,128]{3,2,1,0:T(8,128)}, u32[]{:S(2)}, u32[]{:S(2)}) %all-to-all-start.3) | async-done | bytes 4194336 | tf_op jit(solution)/shard_map/all_to_all | solution.py:38
  170.3 340.4 %while.15 = (s32[]{:T(128)}, f32[128,64,128]{2,1,0:T(8,128)}, f32[128,64,128]{2,1,0:T(8,128)}, f32[8,64,64]{2,0,1:T(8,128)S(1)}, s32[]{:T(128)}, /*index=5*/s32[...) while((s32[]{:T(128)}, f32[128,64,128]{2,1,0:T(8,128)}, ...), condition=%wide.region_3.6_spmd.clone, body=%wide.region_0.5_spmd.clone.sunk | while | flops 4486369280 | bytes 97923816 | solution.py:84
  209.8 5.9 fusion.123
  218.1 8.9 subtract_multiply_fusion.2
  241.6 9.5 fusion.124
  251.1 10.4 scatter_fusion
  261.5 10.3 scatter_fusion.1
  288.2 5.9 fusion.123
  296.4 8.9 subtract_multiply_fusion.2
  319.9 9.5 fusion.124
  329.4 10.3 scatter_fusion
  339.8 10.4 scatter_fusion.1
  366.4 5.9 fusion.123
  374.7 8.9 subtract_multiply_fusion.2
  398.2 9.5 fusion.124
  407.7 10.4 scatter_fusion
  418.1 10.4 scatter_fusion.1
  444.8 5.9 fusion.123
  453.0 8.9 subtract_multiply_fusion.2
  476.5 9.5 fusion.124
  486.1 10.4 scatter_fusion
  496.4 10.4 scatter_fusion.1
  510.7 371.7 %all_to_all.44 = f32[128,1,64,128]{3,2,1,0:T(8,128)} all-to-all(f32[128,1,64,128]{3,2,1,0:T(8,128)} %bitcast.99), channel_id=1, replica_groups=mesh['tm'=16,'rows'=8] {'tm','rows'}, dimensions={0} | all-to-all | bytes 8388608 | tf_op jit(solution)/shard_map/all_to_all | solution.py:93
  882.4 6.1 all-to-all-start.4
  894.8 79.5 %all-reduce.3.cloned.1.call-done = f32[8,64,64]{2,0,1:T(8,128)} async-done(((f32[8,64,64]{2,0,1:T(8,128)}), f32[8,64,64]{2,0,1:T(8,128)}) %all-reduce.3.cloned.1.call-update) | async-done | bytes 131088 | tf_op jit(solution)/shard_map/psum | solution.py:113
  977.1 155.0 %all-reduce.5.cloned.1.call-done = f32[64,64,64]{2,1,0:T(8,128)} async-done(((f32[64,64,64]{2,1,0:T(8,128)}), f32[64,64,64]{2,1,0:T(8,128)}) %all-reduce.5.cloned.1.call-update) | async-done | bytes 1048592 | tf_op jit(solution)/shard_map/psum | solution.py:116
  1140.1 5.8 fusion.43
  (123 shorter events, 187.0 us)
Async XLA Ops:
  7.2 106.3 %copy-start = (f32[64,64,64]{2,1,0:T(8,128)S(1)}, f32[64,64,64]{2,1,0:T(8,128)}, u32[]{:S(2)}) copy-start(f32[64,64,64]{2,1,0:T(8,128)} %param.27) | copy-start | bytes 3145732
  7.2 29.5 %copy-start.4 = (f32[8,64,128]{2,1,0:T(8,128)S(1)}, f32[8,64,128]{2,1,0:T(8,128)}, u32[]{:S(2)}) copy-start(f32[8,64,128]{2,1,0:T(8,128)} %param.25) | copy-start | bytes 786436
  8.7 20.9 %all-to-all-start.1 = ((s32[128,1,1]{2,1,0:T(1,128)}), s32[128,1,1]{2,1,0:T(1,128)S(1)}, u32[]{:S(2)}, u32[]{:S(2)}) async-start(s32[128,1,1]{2,1,0:T(1,128)} %copy.31), calls=%async_computation.1 | async-start | bytes 131072 | tf_op jit(solution)/shard_map/all_to_all | solution.py:35
  29.7 14.3 %all-to-all-start = ((s32[128,1,1]{2,1,0:T(1,128)}), s32[128,1,1]{2,1,0:T(1,128)S(1)}, u32[]{:S(2)}, u32[]{:S(2)}) async-start(s32[128,1,1]{2,1,0:T(1,128)} %copy.30), calls=%async_computation | async-start | bytes 131072 | tf_op jit(solution)/shard_map/all_to_all | solution.py:34
  44.0 12.6 %copy-start.5 = (f32[8,64,128]{2,1,0:T(8,128)S(1)}, f32[8,64,128]{2,1,0:T(8,128)}, u32[]{:S(2)}) copy-start(f32[8,64,128]{2,1,0:T(8,128)} %param.24) | copy-start | bytes 786436
  44.0 62.8 %all-to-all-start.2 = ((f32[128,1,64,128]{3,2,1,0:T(8,128)}), f32[128,1,64,128]{3,2,1,0:T(8,128)}, u32[]{:S(2)}, u32[]{:S(2)}) async-start(f32[128,1,64,128]{3,2,1,0:T(8,128)} %bitcast_select_fusion.1), calls=%async_computation.2 | async-start | bytes 8388608 | tf_op jit(solution)/shard_map/all_to_all | solution.py:39
  63.9 49.6 %copy-start.8 = (f32[8,64]{1,0:T(8,128)S(1)}, f32[8,64]{1,0:T(8,128)}, u32[]{:S(2)}) copy-start(f32[8,64]{1,0:T(8,128)} %param.26) | copy-start | bytes 6148
  106.8 58.6 %all-to-all-start.3 = ((f32[128,1,64,128]{3,2,1,0:T(8,128)}), f32[128,1,64,128]{3,2,1,0:T(8,128)}, u32[]{:S(2)}, u32[]{:S(2)}) async-start(f32[128,1,64,128]{3,2,1,0:T(8,128)} %bitcast_select_fusion), calls=%async_computation.3 | async-start | bytes 8388608 | tf_op jit(solution)/shard_map/all_to_all | solution.py:38
  209.8 5.9 copy-start.1
  209.8 5.9 copy-start.3
  227.0 3.9 copy-start.2
  288.2 5.9 copy-start.1
  288.2 5.9 copy-start.3
  305.3 3.9 copy-start.2
  366.4 5.9 copy-start.1
  366.4 5.9 copy-start.3
  383.6 3.9 copy-start.2
  444.8 5.9 copy-start.1
  444.8 5.9 copy-start.3
  461.9 3.9 copy-start.2
  510.7 377.9 %copy-start.7 = (f32[8,64,64]{2,0,1:T(8,128)}, f32[8,64,64]{2,0,1:T(8,128)S(1)}, u32[]{:S(2)}) copy-start(f32[8,64,64]{2,0,1:T(8,128)S(1)} %get-tuple-element.83) | copy-start | bytes 393220
  882.4 257.6 %all-to-all-start.4 = ((f32[128,1,64,128]{3,2,1,0:T(8,128)}), f32[128,1,64,128]{3,2,1,0:T(8,128)}, u32[]{:S(2)}, u32[]{:S(2)}) async-start(f32[128,1,64,128]{3,2,1,0:T(8,128)} %bitcast.100), calls=%async_computation.4 | async-start | bytes 8388608 | tf_op jit(solution)/shard_map/all_to_all | solution.py:86
  893.4 81.0 %all-reduce.3.cloned.1.call-start = ((), (), s32[]{:S(2)}) async-start(), calls=%async_computation.6 | async-start | bytes 524288 | tf_op jit(solution)/shard_map/psum | solution.py:113
  894.1 238.0 %all-reduce.5.cloned.1.call-start = ((), (), s32[]{:S(2)}) async-start(), calls=%async_computation.7 | async-start | bytes 4194304 | tf_op jit(solution)/shard_map/psum | solution.py:116
  1132.1 3.4 copy-start.6
Sparse Core Ops, SparseCore 0:
  897.1 77.2 all-reduce.2
  980.6 151.5 all-reduce.4
where the time goes:
time: 1160 us; the launch traced here: 1150 us
  blocking collectives  372 us (32%)
  waiting for transfers between devices  334 us (29%)
  matrix products  196 us (17%)
  other arithmetic  106 us (9%)
  local copies, waits for them, and re-layouts  65 us (6%)
  starting transfers between devices  38.8 us (3%)
  loops' own time  27.6 us (2%)
  between operations  15.1 us (1%)
    all_to_all x1, blocking collectives, shards(): lax.all_to_all(slot_right.reshape(owners, slot_cap, rank, width), ('tm',...  372 us
    psum x1, waiting for transfers between devices, shards(): core_total = lax.psum(own_term, ('tm', 'rows'))  155 us
    psum x1, waiting for transfers between devices, shards(): slice_total = lax.psum(step_sums, 'rows')  79.5 us
    all_to_all x1, waiting for transfers between devices, shards(): lax.all_to_all(found_user, ('tm', 'rows'), split_axis=0, concat_axis=0, t...  46.9 us
    all_to_all x1, waiting for transfers between devices, shards(): lax.all_to_all(found_item, ('tm', 'rows'), split_axis=0, concat_axis=0, t...  42.8 us
    scatter-add x4, other arithmetic, one_block(): grad_right = grad_right.at[slots_item].add(grad_v)  41.5 us
    scatter-add x4, other arithmetic, one_block(): grad_left = grad_left.at[slots_user].add(grad_u)  41.5 us
    dot_general x4, matrix products, one_block(): grad_u = jnp.einsum('tij,tpj->tpi', resid, mixed, precision=HIGH)  38.2 us
  transfers between devices with their start and end apart: 7, of which 5 were waited for; matrix products, arithmetic and copies ran while one was open for 4% of the time, Pallas kernels for 0%

commit v1 on v0

v1 whole, which is shorter than its diff:
```python
import functools

import jax
import jax.numpy as jnp
from jax import lax
from jax.experimental import pallas as pl
from jax.experimental.pallas import tpu as pltpu
from jax.sharding import PartitionSpec as P

HIGH = lax.Precision.HIGHEST
user_scale = 0.125
time_scale = 1.0 / 2048.0
core_scale = 1.0 / 4096.0

BF = jnp.bfloat16
F32 = jnp.float32
AXES = ("tm", "rows")
cat = jnp.concatenate


def split(x):
    hi = x.astype(BF)
    lo = (x - hi.astype(F32)).astype(BF)
    return hi, lo


def mul(a, b):
    return lax.dot_general(a, b, (((1,), (0,)), ((), ())), preferred_element_type=F32)


def mul_t(a, b):
    return lax.dot_general(a, b, (((1,), (1,)), ((), ())), preferred_element_type=F32)


def tiles_kernel(
    group, slots_user, slots_item, steps, count,
    values, users, items, cores,
    grad_left, grad_right, sums,
    left_t, left, right, core_hl, core_t,
):
    rank = users.shape[1]
    width = users.shape[2]
    block = pl.program_id(0)
    live_count = count[0]

    @pl.when(block == 0)
    def _():
        grad_left[...] = jnp.zeros_like(grad_left)
        grad_right[...] = jnp.zeros_like(grad_right)
        sums[...] = jnp.zeros_like(sums)

        def prep(k, carry):
            x = users[k]
            left[k] = cat(split(x), 0)
            left_t[k] = cat(split(x.T), 1)
            right[k] = cat(split(items[k]), 0)
            return carry

        lax.fori_loop(0, users.shape[0], prep, 0, unroll=4)

        def prep_core(k, carry):
            x = cores[k]
            core_hl[k] = cat(split(x), 1)
            core_t[k] = cat(split(x.T), 1)
            return carry

        lax.fori_loop(0, cores.shape[0], prep_core, 0)

    @pl.when(block * group < live_count)
    def _():
        span = range(group)
        tile = [block * group + t for t in span]
        user = [slots_user[k] for k in tile]
        item = [slots_item[k] for k in tile]
        step = [steps[k] for k in tile]
        rights = [right[v] for v in item]
        mixed = []
        for t in span:
            hi, lo = rights[t][:rank], rights[t][rank:]
            c = core_hl[step[t]]
            mixed.append(mul(cat([c, c], 1), cat([hi, hi, lo, lo], 0)))
        mixed = [split(m) for m in mixed]
        guess = []
        for t in span:
            hi, lo = mixed[t]
            x = left_t[user[t]]
            guess.append(mul(cat([x, x], 1), cat([hi, hi, lo, lo], 0)))
        resid = [
            split(jnp.where(tile[t] < live_count, guess[t] - values[t].astype(F32), 0.0))
            for t in span
        ]
        inner = []
        for t in span:
            a = mul(left[user[t]], cat(resid[t], 1))
            inner.append((a[:rank, :width] + a[:rank, width:]) + (a[rank:, :width] + a[rank:, width:]))
        grad_u = []
        for t in span:
            a = mul_t(cat(mixed[t], 0), cat(resid[t], 0))
            grad_u.append((a[:rank, :width] + a[:rank, width:]) + (a[rank:, :width] + a[rank:, width:]))
        inner = [split(x) for x in inner]
        grad_v = []
        for t in span:
            hi, lo = inner[t]
            c = core_t[step[t]]
            grad_v.append(mul(cat([c, c], 1), cat([hi, hi, lo, lo], 0)))
        dcore = []
        for t in span:
            a = mul_t(cat(inner[t], 0), rights[t])
            a = a[:rank] + a[rank:]
            dcore.append(a[:, :rank] + a[:, rank:])
        for t in span:
            grad_left[user[t]] += grad_u[t]
            grad_right[item[t]] += grad_v[t]
            sums[step[t]] += dcore[t]


def tiles_call(slots_user, slots_item, steps, count, values, users, items, cores):
    group = 16
    slots, width = values.shape[0], values.shape[1]
    rank = users.shape[1]

    def whole(shape):
        return pl.BlockSpec(shape, lambda b, *_: (0,) * len(shape), pipeline_mode=pl.Buffered(1))

    def values_at(b, su, si, st, cnt):
        last = jnp.maximum((cnt[0] + group - 1) // group - 1, 0)
        return (jnp.minimum(b, last), 0, 0)

    return pl.pallas_call(
        functools.partial(tiles_kernel, group),
        grid_spec=pltpu.PrefetchScalarGridSpec(
            num_scalar_prefetch=4,
            grid=(slots // group,),
            in_specs=[
                pl.BlockSpec((group, width, width), values_at),
                whole(users.shape),
                whole(items.shape),
                whole(cores.shape),
            ],
            out_specs=[whole(users.shape), whole(items.shape), whole(cores.shape)],
            scratch_shapes=[
                pltpu.VMEM((users.shape[0], width, 2 * rank), BF),
                pltpu.VMEM((users.shape[0], 2 * rank, width), BF),
                pltpu.VMEM((items.shape[0], 2 * rank, width), BF),
                pltpu.VMEM((cores.shape[0], rank, 2 * rank), BF),
                pltpu.VMEM((cores.shape[0], rank, 2 * rank), BF),
            ],
        ),
        out_shape=[
            jax.ShapeDtypeStruct(users.shape, F32),
            jax.ShapeDtypeStruct(items.shape, F32),
            jax.ShapeDtypeStruct(cores.shape, F32),
        ],
        compiler_params=pltpu.CompilerParams(
            vmem_limit_bytes=60 * 2**20, dimension_semantics=("arbitrary",)
        ),
        name="tiles",
    )(slots_user, slots_item, steps, count, values, users, items, cores)


def owner_kernel(group, held, back, out):
    block = pl.program_id(0)

    @pl.when(block == 0)
    def _():
        out[...] = jnp.zeros_like(out)

    for t in range(group):
        out[held[block * group + t]] += back[t]

    @pl.when(block == pl.num_programs(0) - 1)
    def _():
        out[...] = out[...] * user_scale


def owner_sum(held, back, blocks_own):
    group = 16
    total, rank, width = back.shape
    return pl.pallas_call(
        functools.partial(owner_kernel, group),
        grid_spec=pltpu.PrefetchScalarGridSpec(
            num_scalar_prefetch=1,
            grid=(total // group,),
            in_specs=[pl.BlockSpec((group, rank, width), lambda b, *_: (b, 0, 0))],
            out_specs=pl.BlockSpec((blocks_own, rank, width), lambda b, *_: (0, 0, 0)),
        ),
        out_shape=jax.ShapeDtypeStruct((blocks_own, rank, width), F32),
        compiler_params=pltpu.CompilerParams(dimension_semantics=("arbitrary",)),
        name="owners",
    )(held, back)


def to_all(x):
    return lax.all_to_all(x, AXES, split_axis=0, concat_axis=0, tiled=True)


def shards(
    tile_values,
    tile_users,
    tile_items,
    tile_steps,
    tile_count,
    users_ask,
    items_ask,
    user_factor,
    item_factor,
    time_factor,
    core,
):
    rank = user_factor.shape[1]
    width = user_factor.shape[2]
    blocks_own = user_factor.shape[0]
    step_count = time_factor.shape[0]
    asks = to_all(cat([users_ask, items_ask], 1))
    held_user, held_item = asks[:, 0], asks[:, 1]
    found_user = user_factor.at[held_user].get(mode="promise_in_bounds")
    found_item = item_factor.at[held_item].get(mode="promise_in_bounds")
    users = to_all(found_user)
    items = to_all(found_item)
    step_cores = jnp.einsum("pqr,sr->spq", core, time_factor, precision=HIGH)
    slot_left, slot_right, step_sums = tiles_call(
        tile_users, tile_items, tile_steps, tile_count, tile_values, users, items, step_cores
    )
    mine = lax.all_to_all(
        step_sums.reshape(step_count, rank * rank), "rows", split_axis=0, concat_axis=0, tiled=True
    )
    total = jnp.sum(mine, axis=0)
    every_time = lax.all_gather(time_factor, "tm", axis=0, tiled=True)
    every = lax.all_gather(total, AXES, axis=0, tiled=False)
    slice_at = lax.axis_index("tm") * step_count
    own = lax.dynamic_slice_in_dim(every, slice_at, step_count, 0)
    grad_time = time_scale * jnp.einsum(
        "sk,kr->sr", own, core.reshape(rank * rank, rank), precision=HIGH
    )
    grad_core = core_scale * jnp.einsum("sk,sr->kr", every, every_time, precision=HIGH)
    grad_core = grad_core.reshape(rank, rank, rank)
    back_left = to_all(slot_left)
    back_right = to_all(slot_right)
    grad_users = owner_sum(held_user, back_left, blocks_own)
    grad_items = owner_sum(held_item, back_right, blocks_own)
    return (grad_users, grad_items, grad_time, grad_core)


def solution(mesh):
    in_specs = (
        P(AXES, None, None),
        P(AXES),
        P(AXES),
        P(AXES),
        P(AXES),
        P(AXES, None),
        P(AXES, None),
        P(AXES, None, None),
        P(AXES, None, None),
        P("tm", None),
        P(),
    )
    out_specs = (P(AXES, None, None), P(AXES, None, None), P("tm", None), P())
    return jax.shard_map(shards, mesh=mesh, in_specs=in_specs, out_specs=out_specs, check_vma=False)
```

time: 1160 us -> 411 us (0.35)
  waiting for transfers between devices: 334 us -> 118 us
  matrix products: 196 us -> 10.5 us
  blocking collectives: 372 us -> 196 us
  other arithmetic: 106 us -> 2.27 us
  local copies, waits for them, and re-layouts: 65 us -> 13.2 us
  Pallas kernels: 0 us -> 38.4 us
  loops' own time: 27.6 us -> 0 us
  starting transfers between devices: 38.8 us -> 17.8 us
    all_to_all x1 -> x3, blocking collectives: 372 us -> 135 us  [the longest x2 79.3 us: to_all(): return lax.all_to_all(x, AXES, split_axis=0, concat_axis=0, tiled=True)]
    psum x2 -> x0, waiting for transfers between devices: 235 us -> none  [the longest x1 155 us: shards(): core_total = lax.psum(own_term, ('tm', 'rows'))]
    dot_general x40 -> x2, matrix products: 191 us -> 5.52 us  [the longest x1 2.89 us: shards(): jnp.einsum('sk,sr->kr', every, every_time, precision=HIGH)]
    scatter-add x8 -> x0, other arithmetic: 82.9 us -> none  [the longest x4 41.5 us: one_block(): grad_right = grad_right.at[slots_item].add(grad_v)]
    all_gather x0 -> x1, blocking collectives: none -> 60.8 us  [shards(): every_time = lax.all_gather(time_factor, 'tm', axis=0, tiled=True)]
    pallas_call x0 -> x3, Pallas kernels: none -> 38.4 us  [the longest x1 25.9 us: tiles_call(): pl.pallas_call(functools.partial(tiles_kernel, group), grid_spec=pltpu.Pr...]
    gather x10 -> x2, local copies, waits for them, and re-layouts: 39.1 us -> 6.46 us  [the longest x1 3.69 us: shards(): found_user = user_factor.at[held_user].get(mode='promise_in_bounds')]
    another operation x1 -> x0, loops' own time: 27.6 us -> none  [shards(): lax.fori_loop(0, block_total, one_block, start_carry)]
  transfers between devices with their start and end apart: 7 -> 4, of which waited for: 5 -> 3; matrix products, arithmetic and copies ran while one was open for 4% -> 2% of each run, Pallas kernels for 0% -> 3%
where the time goes in v1:
time: 411 us; the launch traced here: 410 us
  blocking collectives  196 us (48%)
  waiting for transfers between devices  118 us (29%)
  Pallas kernels  38.4 us (9%)
  starting transfers between devices  17.8 us (4%)
  between operations  14.8 us (4%)
  local copies, waits for them, and re-layouts  13.2 us (3%)
  matrix products  10.5 us (3%)
    all_to_all x3, waiting for transfers between devices, to_all(): return lax.all_to_all(x, AXES, split_axis=0, concat_axis=0, tiled=True)  96 us
    all_to_all x2, blocking collectives, to_all(): return lax.all_to_all(x, AXES, split_axis=0, concat_axis=0, tiled=True)  79.3 us
    all_gather x1, blocking collectives, shards(): every_time = lax.all_gather(time_factor, 'tm', axis=0, tiled=True)  60.8 us
    all_to_all x1, blocking collectives, shards(): lax.all_to_all(step_sums.reshape(step_count, rank * rank), 'rows', split_...  55.4 us
    pallas_call x1, Pallas kernels, tiles_call(): pl.pallas_call(functools.partial(tiles_kernel, group), grid_spec=pltpu.Pr...  25.9 us
    all_gather x1, waiting for transfers between devices, shards(): every = lax.all_gather(total, AXES, axis=0, tiled=False)  21.8 us
    all_to_all x3, starting transfers between devices, to_all(): return lax.all_to_all(x, AXES, split_axis=0, concat_axis=0, tiled=True)  17.7 us
    pallas_call x2, Pallas kernels, owner_sum(): pl.pallas_call(functools.partial(owner_kernel, group), grid_spec=pltpu.Pr...  12.5 us
  transfers between devices with their start and end apart: 4, of which 3 were waited for; matrix products, arithmetic and copies ran while one was open for 2% of the time, Pallas kernels for 3%

profile of v1, /device:TPU:1, one launch (start us, length us, event | category | flops | bytes accessed | tf_op | source)
XLA Modules:
  0.0 410.2 jit_solution(3401384593230270765)
XLA Ops:
  7.2 0.0 copy-start
  7.2 0.8 pad_add_fusion
  8.0 0.1 copy.27
  8.1 20.8 %all_to_all.42 = s32[128,1,2]{2,1,0:T(1,128)S(1)} all-to-all(s32[128,1,2]{2,1,0:T(1,128)S(1)} %bitcast.14), channel_id=1, replica_groups=mesh['tm'=16,'rows'=8] {'tm','rows'}, dimensions={0} | all-to-all | bytes 2048 | tf_op jit(solution)/shard_map/all_to_all | solution.py:194
  28.9 0.7 slice_reduce_fusion
  29.7 3.7 gather_fusion
  33.3 5.6 %all-to-all-start.1 = ((f32[128,64,128]{2,1,0:T(8,128)}), f32[128,64,128]{2,1,0:T(8,128)}, u32[]{:S(2)}, u32[]{:S(2)}) async-start(f32[128,64,128]{2,1,0:T(8,128)} %gather_fusion), calls=%async_computation.1 | async-start | bytes 8388608 | tf_op jit(solution)/shard_map/all_to_all | solution.py:194
  38.9 0.0 copy-done.1
  38.9 2.8 gather_fusion.1
  41.7 49.9 %all-to-all-done.1.users = f32[128,64,128]{2,1,0:T(8,128)} async-done(((f32[128,64,128]{2,1,0:T(8,128)}), f32[128,64,128]{2,1,0:T(8,128)}, u32[]{:S(2)}, u32[]{:S(2)}) %all-to-all-start.1) | async-done | bytes 4194336 | tf_op jit(solution)/shard_map/all_to_all | solution.py:194
  91.6 6.1 %all-to-all-start.2 = ((f32[128,64,128]{2,1,0:T(8,128)}), f32[128,64,128]{2,1,0:T(8,128)}, u32[]{:S(2)}, u32[]{:S(2)}) async-start(f32[128,64,128]{2,1,0:T(8,128)} %gather_fusion.1), calls=%async_computation.2 | async-start | bytes 8388608 | tf_op jit(solution)/shard_map/all_to_all | solution.py:194
  97.7 0.0 copy-done
  97.7 4.9 %fusion.3 = f32[8,64,64]{2,0,1:T(8,128)S(1)} fusion(f32[64,64,64]{2,1,0:T(8,128)S(1)} %copy-done, f32[8,64]{1,0:T(8,128)S(1)} %copy-done.2), kind=kOutput, calls=%fused_computation.13 | convolution fusion | flops 25165824 | bytes 1181696 | tf_op jit(solution)/shard_map/pqr,sr->spq/dot_general | solution.py:220
  102.7 0.8 copy.28.cores
  104.1 46.1 %all-to-all-done.2.items = f32[128,64,128]{2,1,0:T(8,128)} async-done(((f32[128,64,128]{2,1,0:T(8,128)}), f32[128,64,128]{2,1,0:T(8,128)}, u32[]{:S(2)}, u32[]{:S(2)}) %all-to-all-start.2) | async-done | bytes 4194336 | tf_op jit(solution)/shard_map/all_to_all | solution.py:194
  150.3 25.9 %tiles.1 = (f32[128,64,128]{2,1,0:T(8,128)}, f32[128,64,128]{2,1,0:T(8,128)}, f32[8,64,64]{2,1,0:T(8,128)}) custom-call(s32[512]{0:T(512)} %slots_user.1, s32[512]{0:T(512)} %slots_item.1, s32[512]{0:T(512)} %steps.1, s32[1]{0:T(128)S(6)} %copy.32.count, bf16[512,128,128]{2,1,0:T(8,128)(2,1)} %values.1, f32[128,64,128]{2,1,0:T(8,128)} %all-to-all-done.1.users, ...), custom_call_target="tpu_custom_call" | custom-call | tf_op jit(solution)/shard_map/tiles/pallas_call | solution.py:129
  176.2 1.1 all_to_all.35
  177.3 55.4 %all_to_all.43 = f32[8,1,4096]{2,1,0:T(1,128)S(1)} all-to-all(f32[8,1,4096]{2,1,0:T(1,128)S(1)} %all_to_all.35), channel_id=1, replica_groups=mesh['tm'=16,'rows'=8] {'rows'}, dimensions={0} | all-to-all | bytes 262144 | tf_op jit(solution)/shard_map/all_to_all | solution.py:224
  232.7 58.5 %all_to_all.44.back = f32[128,64,128]{2,1,0:T(8,128)} all-to-all(f32[128,64,128]{2,1,0:T(8,128)} %get-tuple-element.8), channel_id=1, replica_groups=mesh['tm'=16,'rows'=8] {'tm','rows'}, dimensions={0} | all-to-all | bytes 8388608 | tf_op jit(solution)/shard_map/all_to_all | solution.py:194
  291.2 6.0 %all-to-all-start.3 = ((f32[128,64,128]{2,1,0:T(8,128)}), f32[128,64,128]{2,1,0:T(8,128)}, u32[]{:S(2)}, u32[]{:S(2)}) async-start(f32[128,64,128]{2,1,0:T(8,128)} %get-tuple-element.7), calls=%async_computation.3 | async-start | bytes 8388608 | tf_op jit(solution)/shard_map/all_to_all | solution.py:194
  297.3 0.0 all-gather.3.cloned.1.call-start
  297.3 0.7 reduce_sum.9
  298.0 0.0 all-gather.3.cloned.1.call-update
  298.1 60.8 %all_gather.11 = f32[128,64]{1,0:T(8,128)S(1)} all-gather(f32[8,64]{1,0:T(8,128)S(1)} %copy-done.2), channel_id=1, replica_groups=mesh['tm'=16,'rows'=8] {'tm'}, dimensions={0}, use_global_device_ids=true | all-gather | bytes 34816 | tf_op jit(solution)/shard_map/all_gather | solution.py:228
  358.9 6.2 %owners.3 = f32[8,64,128]{2,1,0:T(8,128)} custom-call(s32[128]{0:T(128)} %get-tuple-element.26.held, f32[128,64,128]{2,1,0:T(8,128)} %all_to_all.44.back), custom_call_target="tpu_custom_call" | custom-call | tf_op jit(solution)/shard_map/owners/pallas_call | solution.py:179
  365.1 0.0 all-to-all-done.3.back
  365.1 6.2 %owners.2 = f32[8,64,128]{2,1,0:T(8,128)} custom-call(s32[128]{0:T(128)} %get-tuple-element.29.held, f32[128,64,128]{2,1,0:T(8,128)} %all-to-all-done.3.back), custom_call_target="tpu_custom_call" | custom-call | tf_op jit(solution)/shard_map/owners/pallas_call | solution.py:179
  371.3 21.8 %all-gather.3.cloned.1.call-done = f32[524288]{0:T(1024)} async-done(((f32[4096]{0:T(1024)}), f32[524288]{0:T(1024)}) %all-gather.3.cloned.1.call-update) | async-done | bytes 2097168 | tf_op jit(solution)/shard_map/all_gather | solution.py:229
  393.2 2.8 reshape.38
  395.9 2.9 convolution_multiply_fusion
  398.8 1.9 copy.31
  400.8 2.6 convolution_multiply_fusion.1
  (5 shorter events, 0.0 us)
Async XLA Ops:
  7.2 90.6 %copy-start = (f32[64,64,64]{2,1,0:T(8,128)S(1)}, f32[64,64,64]{2,1,0:T(8,128)}, u32[]{:S(2)}) copy-start(f32[64,64,64]{2,1,0:T(8,128)} %param.21) | copy-start | bytes 3145732
  33.3 5.6 %copy-start.1 = (f32[8,64,128]{2,1,0:T(8,128)S(1)}, f32[8,64,128]{2,1,0:T(8,128)}, u32[]{:S(2)}) copy-start(f32[8,64,128]{2,1,0:T(8,128)} %param.19) | copy-start | bytes 786436
  33.3 58.2 %all-to-all-start.1 = ((f32[128,64,128]{2,1,0:T(8,128)}), f32[128,64,128]{2,1,0:T(8,128)}, u32[]{:S(2)}, u32[]{:S(2)}) async-start(f32[128,64,128]{2,1,0:T(8,128)} %gather_fusion), calls=%async_computation.1 | async-start | bytes 8388608 | tf_op jit(solution)/shard_map/all_to_all | solution.py:194
  41.7 56.0 %copy-start.2 = (f32[8,64]{1,0:T(8,128)S(1)}, f32[8,64]{1,0:T(8,128)}, u32[]{:S(2)}) copy-start(f32[8,64]{1,0:T(8,128)} %param.20) | copy-start | bytes 6148
  91.6 58.7 %all-to-all-start.2 = ((f32[128,64,128]{2,1,0:T(8,128)}), f32[128,64,128]{2,1,0:T(8,128)}, u32[]{:S(2)}, u32[]{:S(2)}) async-start(f32[128,64,128]{2,1,0:T(8,128)} %gather_fusion.1), calls=%async_computation.2 | async-start | bytes 8388608 | tf_op jit(solution)/shard_map/all_to_all | solution.py:194
  291.2 73.9 %all-to-all-start.3 = ((f32[128,64,128]{2,1,0:T(8,128)}), f32[128,64,128]{2,1,0:T(8,128)}, u32[]{:S(2)}, u32[]{:S(2)}) async-start(f32[128,64,128]{2,1,0:T(8,128)} %get-tuple-element.7), calls=%async_computation.3 | async-start | bytes 8388608 | tf_op jit(solution)/shard_map/all_to_all | solution.py:194
  297.3 95.9 %all-gather.3.cloned.1.call-start = ((), (), s32[]{:S(2)}) async-start(), calls=%async_computation.6 | async-start | bytes 2113536 | tf_op jit(solution)/shard_map/all_gather | solution.py:229
Sparse Core Ops, SparseCore 0:
  301.8 91.2 all-gather.2

commit v2 on v1

v2 whole, which is shorter than its diff:
```python
import functools

import jax
import jax.numpy as jnp
from jax import lax
from jax.experimental import pallas as pl
from jax.experimental.pallas import tpu as pltpu
from jax.sharding import PartitionSpec as P

HIGH = lax.Precision.HIGHEST
user_scale = 0.125
time_scale = 1.0 / 2048.0
core_scale = 1.0 / 4096.0

BF = jnp.bfloat16
F32 = jnp.float32
AXES = ("tm", "rows")
cat = jnp.concatenate
PREP = 8


def split(x):
    hi = x.astype(BF)
    lo = (x - hi.astype(F32)).astype(BF)
    return hi, lo


def mul(a, b):
    return lax.dot_general(a, b, (((1,), (0,)), ((), ())), preferred_element_type=F32)


def mul_t(a, b):
    return lax.dot_general(a, b, (((1,), (1,)), ((), ())), preferred_element_type=F32)


def twice(x):
    return cat([x, x], 1)


def quad(hi, lo):
    return cat([hi, hi, lo, lo], 0)


def pairs(hi, lo):
    return cat([twice(hi), twice(lo)], 0)


def whole(shape):
    return pl.BlockSpec(shape, lambda b, *_: (0,) * len(shape), pipeline_mode=pl.Buffered(1))


def live_block(group):
    def at(b, *scalars):
        last = jnp.maximum((scalars[-1][0] + group - 1) // group - 1, 0)
        return (jnp.minimum(b, last), 0, 0)
    return at


def params():
    return pltpu.CompilerParams(vmem_limit_bytes=60 * 2**20, dimension_semantics=("arbitrary",))


def in_groups(total, size, step):
    def one(g, carry):
        step([g * size + t for t in range(size)])
        return carry
    lax.fori_loop(0, total // size, one, 0)


def item_kernel(group, slots_user, slots_item, steps, count, items, cores, values,
                gram, moved, mixed_out, right, core_hl, gram_sum):
    rank, width = items.shape[1], items.shape[2]
    block = pl.program_id(0)

    @pl.when(block == 0)
    def _():
        def prep(ks):
            out = [cat(split(items[k]), 0) for k in ks]
            for k, x in zip(ks, out):
                right[k] = x
            for k in ks:
                gram_sum[k] = jnp.zeros_like(gram_sum[k])
                moved[k] = jnp.zeros_like(moved[k])
        in_groups(items.shape[0], PREP, prep)
        for k in range(cores.shape[0]):
            core_hl[k] = cat(split(cores[k]), 1)

    @pl.when(block * group < count[0])
    def _():
        span = range(group)
        tile = [block * group + t for t in span]
        user = [slots_user[k] for k in tile]
        mixed = []
        for t in span:
            r = right[slots_item[tile[t]]]
            mixed.append(mul(twice(core_hl[steps[tile[t]]]), quad(r[:rank], r[rank:])))
        mixed = [split(jnp.where(tile[t] < count[0], mixed[t], 0.0)) for t in span]
        both = []
        for t in span:
            v = values[t]
            both.append(mul_t(cat(mixed[t], 1), cat([twice(v), pairs(*mixed[t])], 0)))
        for t in span:
            mixed_out[t] = cat(mixed[t], 0)
        for t in span:
            moved[user[t]] += both[t][:, :width]
            gram_sum[user[t]] += both[t][:, width:]

    @pl.when(block == pl.num_programs(0) - 1)
    def _():
        def finish(ks):
            out = [gram_sum[k] for k in ks]
            out = [cat(split(x[:, :rank] + x[:, rank:]), 1) for x in out]
            for k, x in zip(ks, out):
                gram[k] = x
        in_groups(gram.shape[0], PREP, finish)


def item_call(slots_user, slots_item, steps, count, items, cores, values, group=32):
    slots, width = values.shape[:2]
    held, rank = items.shape[:2]
    return pl.pallas_call(
        functools.partial(item_kernel, group),
        grid_spec=pltpu.PrefetchScalarGridSpec(
            num_scalar_prefetch=4,
            grid=(slots // group,),
            in_specs=[whole(items.shape), whole(cores.shape),
                      pl.BlockSpec((group, width, width), live_block(group))],
            out_specs=[whole((held, rank, 2 * rank)), whole((held, rank, width)),
                       pl.BlockSpec((group, 2 * rank, width), live_block(group)),
                       whole((held, 2 * rank, width))],
            scratch_shapes=[pltpu.VMEM((cores.shape[0], rank, 2 * rank), BF),
                            pltpu.VMEM((held, rank, 2 * rank), F32)],
        ),
        out_shape=[jax.ShapeDtypeStruct((held, rank, 2 * rank), BF),
                   jax.ShapeDtypeStruct((held, rank, width), F32),
                   jax.ShapeDtypeStruct((slots, 2 * rank, width), BF),
                   jax.ShapeDtypeStruct((held, 2 * rank, width), BF)],
        compiler_params=params(),
        cost_estimate=pl.CostEstimate(flops=2 * 10**10, bytes_accessed=5 * 10**7, transcendentals=0),
        name="item_side",
    )(slots_user, slots_item, steps, count, items, cores, values)


def user_grad_kernel(group, users, gram, moved, grad):
    span = range(group)
    out = [mul(twice(gram[t]), quad(*split(users[t]))) for t in span]
    for t in span:
        grad[t] = out[t] - moved[t]


def user_grad_call(users, gram, moved, group=16):
    held, rank, width = users.shape
    block = pl.BlockSpec((group, rank, width), lambda b: (b, 0, 0))
    return pl.pallas_call(
        functools.partial(user_grad_kernel, group),
        grid=(held // group,),
        in_specs=[block, pl.BlockSpec((group, rank, 2 * rank), lambda b: (b, 0, 0)), block],
        out_specs=block,
        out_shape=jax.ShapeDtypeStruct(users.shape, F32),
        compiler_params=params(),
        cost_estimate=pl.CostEstimate(flops=10**9, bytes_accessed=2 * 10**7, transcendentals=0),
        name="user_grad",
    )(users, gram, moved)


def tile_kernel(group, slots_user, slots_item, steps, count, users, right, cores, values, mixed,
                grad, sums, left, core_t, sums_hl):
    rank, width = users.shape[1], users.shape[2]
    block = pl.program_id(0)

    @pl.when(block == 0)
    def _():
        def prep(ks):
            x = [split(users[k]) for k in ks]
            h = [mul_t(cat(y, 1), pairs(*y)) for y in x]
            h = [cat(split(y[:, :rank] + y[:, rank:]), 1) for y in h]
            for k, y, z in zip(ks, x, h):
                left[k] = cat([-y[0], -y[1], z], 1)
                grad[k] = jnp.zeros_like(grad[k])
        in_groups(users.shape[0], PREP, prep)
        for k in range(cores.shape[0]):
            core_t[k] = cat(split(cores[k].T), 1)
        sums_hl[...] = jnp.zeros_like(sums_hl)

    @pl.when(block * group < count[0])
    def _():
        span = range(group)
        tile = [block * group + t for t in span]
        item = [slots_item[k] for k in tile]
        step = [steps[k] for k in tile]
        inner = []
        for t in span:
            x = left[slots_user[tile[t]]]
            v, m = values[t], mixed[t]
            inner.append(mul(cat([x, x[:, 2 * width:]], 1), cat([v, v, quad(m[:rank], m[rank:])], 0)))
        inner = [split(jnp.where(tile[t] < count[0], inner[t], 0.0)) for t in span]
        grad_v = [mul(twice(core_t[step[t]]), quad(*inner[t])) for t in span]
        dcore = []
        for t in span:
            a = mul_t(cat(inner[t], 0), right[item[t]])
            dcore.append(a[:rank] + a[rank:])
        for t in span:
            grad[item[t]] += grad_v[t]
            sums_hl[step[t]] += dcore[t]

    @pl.when(block == pl.num_programs(0) - 1)
    def _():
        for k in range(sums.shape[0]):
            a = sums_hl[k]
            sums[k] = a[:, :rank] + a[:, rank:]


def tile_call(slots_user, slots_item, steps, count, users, right, cores, values, mixed, group=32):
    slots, width = values.shape[:2]
    held, rank = users.shape[:2]
    return pl.pallas_call(
        functools.partial(tile_kernel, group),
        grid_spec=pltpu.PrefetchScalarGridSpec(
            num_scalar_prefetch=4,
            grid=(slots // group,),
            in_specs=[whole(users.shape), whole(right.shape), whole(cores.shape),
                      pl.BlockSpec((group, width, width), live_block(group)),
                      pl.BlockSpec((group, 2 * rank, width), live_block(group))],
            out_specs=[whole((held, rank, width)), whole(cores.shape)],
            scratch_shapes=[pltpu.VMEM((held, rank, 2 * width + 2 * rank), BF),
                            pltpu.VMEM((cores.shape[0], rank, 2 * rank), BF),
                            pltpu.VMEM((cores.shape[0], rank, 2 * rank), F32)],
        ),
        out_shape=[jax.ShapeDtypeStruct((held, rank, width), F32),
                   jax.ShapeDtypeStruct(cores.shape, F32)],
        compiler_params=params(),
        cost_estimate=pl.CostEstimate(flops=3 * 10**10, bytes_accessed=5 * 10**7, transcendentals=0),
        name="tile_side",
    )(slots_user, slots_item, steps, count, users, right, cores, values, mixed)

def owner_kernel(group, held, back, out):
    block = pl.program_id(0)

    @pl.when(block == 0)
    def _():
        out[...] = jnp.zeros_like(out)

    for t in range(group):
        out[held[block * group + t]] += back[t]

    @pl.when(block == pl.num_programs(0) - 1)
    def _():
        out[...] = out[...] * user_scale


def owner_sum(held, back, blocks_own):
    group = 16
    total, rank, width = back.shape
    return pl.pallas_call(
        functools.partial(owner_kernel, group),
        grid_spec=pltpu.PrefetchScalarGridSpec(
            num_scalar_prefetch=1,
            grid=(total // group,),
            in_specs=[pl.BlockSpec((group, rank, width), lambda b, *_: (b, 0, 0))],
            out_specs=pl.BlockSpec((blocks_own, rank, width), lambda b, *_: (0, 0, 0)),
        ),
        out_shape=jax.ShapeDtypeStruct((blocks_own, rank, width), F32),
        compiler_params=pltpu.CompilerParams(dimension_semantics=("arbitrary",)),
        name="owners",
    )(held, back)


def to_all(x):
    return lax.all_to_all(x, AXES, split_axis=0, concat_axis=0, tiled=True)


def shards(
    tile_values,
    tile_users,
    tile_items,
    tile_steps,
    tile_count,
    users_ask,
    items_ask,
    user_factor,
    item_factor,
    time_factor,
    core,
):
    rank = user_factor.shape[1]
    width = user_factor.shape[2]
    blocks_own = user_factor.shape[0]
    step_count = time_factor.shape[0]
    count_tm = lax.axis_size("tm")
    count_rows = lax.axis_size("rows")
    owners = count_tm * count_rows
    asks = to_all(cat([users_ask, items_ask], 1))
    held_user, held_item = asks[:, 0], asks[:, 1]
    found_item = item_factor.at[held_item].get(mode="promise_in_bounds")
    items = to_all(found_item)
    found_user = user_factor.at[held_user].get(mode="promise_in_bounds")
    step_cores = jnp.einsum("pqr,sr->spq", core, time_factor, precision=HIGH)
    found_user, items, step_cores = lax.optimization_barrier((found_user, items, step_cores))
    users = to_all(found_user)
    gram, moved, mixed, right = item_call(
        tile_users, tile_items, tile_steps, tile_count, items, step_cores, tile_values
    )
    slot_left = user_grad_call(users, gram, moved)
    users, slot_left = lax.optimization_barrier((users, slot_left))
    back_left = to_all(slot_left)
    slot_right, step_sums = tile_call(
        tile_users, tile_items, tile_steps, tile_count, users, right, step_cores, tile_values, mixed
    )
    part = rank * rank // owners
    parts = step_sums.reshape(step_count, owners, part).transpose(1, 0, 2)
    row = lax.dynamic_slice_in_dim(time_factor, lax.axis_index("rows"), 1, 0)
    row = jnp.broadcast_to(jnp.pad(row, ((0, 0), (0, width - rank)))[None], (owners, 1, width))
    blank = jnp.zeros((owners, 1, width), F32)
    sent = cat([parts.reshape(owners, -1, width), row, blank], 1)
    sent, back_left = lax.optimization_barrier((sent, back_left))
    got = to_all(sent)
    got, slot_right, step_sums = lax.optimization_barrier((got, slot_right, step_sums))
    back_right = to_all(slot_right)
    some = got[:, : step_count * part // width].reshape(count_tm, count_rows, step_count, part)
    some = jnp.sum(some, axis=1).reshape(count_tm * step_count, part)
    every_time = got[:, step_count * part // width, :rank]
    own = core_scale * jnp.einsum("sk,sr->kr", some, every_time, precision=HIGH)
    grad_core = lax.all_gather(own, AXES, axis=0, tiled=True).reshape(rank, rank, rank)
    own_time = jnp.einsum("spq,pqr->sr", step_sums, core, precision=HIGH)
    grad_time = time_scale * lax.psum(own_time, "rows")
    grad_users = owner_sum(held_user, back_left, blocks_own)
    grad_items = owner_sum(held_item, back_right, blocks_own)
    return (grad_users, grad_items, grad_time, grad_core)


def solution(mesh):
    in_specs = (
        P(AXES, None, None),
        P(AXES),
        P(AXES),
        P(AXES),
        P(AXES),
        P(AXES, None),
        P(AXES, None),
        P(AXES, None, None),
        P(AXES, None, None),
        P("tm", None),
        P(),
    )
    out_specs = (P(AXES, None, None), P(AXES, None, None), P("tm", None), P())
    return jax.shard_map(shards, mesh=mesh, in_specs=in_specs, out_specs=out_specs, check_vma=False)
```

time: 411 us -> 353 us (0.86)
  blocking collectives: 196 us -> 83.6 us
  waiting for transfers between devices: 118 us -> 145 us
  Pallas kernels: 38.4 us -> 63.6 us
  starting transfers between devices: 17.8 us -> 23.3 us
    all_gather x1 -> x0, blocking collectives: 60.8 us -> none  [shards(): every_time = lax.all_gather(time_factor, 'tm', axis=0, tiled=True)]
    all_to_all x1 -> x0, blocking collectives: 55.4 us -> none  [shards(): lax.all_to_all(step_sums.reshape(step_count, rank * rank), 'rows', split_...]
    psum x0 -> x1, blocking collectives: none -> 46.5 us  [shards(): grad_time = time_scale * lax.psum(own_time, 'rows')]
    all_to_all x2, blocking collectives: 79.3 us -> 37.1 us  [to_all(): return lax.all_to_all(x, AXES, split_axis=0, concat_axis=0, tiled=True)]
    pallas_call x1 -> x3, Pallas kernels: 25.9 us -> 51.1 us  [the longest x1 22.3 us: tile_call(): pl.pallas_call(functools.partial(tile_kernel, group), grid_spec=pltpu.Pre...]
    all_gather x1, waiting for transfers between devices: 21.8 us -> 39.9 us  [shards(): lax.all_gather(own, AXES, axis=0, tiled=True).reshape(rank, rank, rank)]
    all_to_all x3 -> x4, waiting for transfers between devices: 96 us -> 105 us  [to_all(): return lax.all_to_all(x, AXES, split_axis=0, concat_axis=0, tiled=True)]
    all_to_all x3 -> x4, starting transfers between devices: 17.7 us -> 23.2 us  [to_all(): return lax.all_to_all(x, AXES, split_axis=0, concat_axis=0, tiled=True)]
  transfers between devices with their start and end apart: 4 -> 5, of which waited for: 3 -> 4; matrix products, arithmetic and copies ran while one was open for 2% -> 4% of each run, Pallas kernels for 3% -> 14%
where the time goes in v2:
time: 353 us; the launch traced here: 352 us
  waiting for transfers between devices  145 us (41%)
  blocking collectives  83.6 us (24%)
  Pallas kernels  63.6 us (18%)
  starting transfers between devices  23.3 us (7%)
  between operations  14.8 us (4%)
  local copies, waits for them, and re-layouts  12.4 us (4%)
  matrix products  7.04 us (2%)
    all_to_all x4, waiting for transfers between devices, to_all(): return lax.all_to_all(x, AXES, split_axis=0, concat_axis=0, tiled=True)  105 us
    psum x1, blocking collectives, shards(): grad_time = time_scale * lax.psum(own_time, 'rows')  46.5 us
    all_gather x1, waiting for transfers between devices, shards(): lax.all_gather(own, AXES, axis=0, tiled=True).reshape(rank, rank, rank)  39.9 us
    all_to_all x2, blocking collectives, to_all(): return lax.all_to_all(x, AXES, split_axis=0, concat_axis=0, tiled=True)  37.1 us
    all_to_all x4, starting transfers between devices, to_all(): return lax.all_to_all(x, AXES, split_axis=0, concat_axis=0, tiled=True)  23.2 us
    pallas_call x1, Pallas kernels, tile_call(): pl.pallas_call(functools.partial(tile_kernel, group), grid_spec=pltpu.Pre...  22.3 us
    pallas_call x1, Pallas kernels, item_call(): pl.pallas_call(functools.partial(item_kernel, group), grid_spec=pltpu.Pre...  19.9 us
    pallas_call x2, Pallas kernels, owner_sum(): pl.pallas_call(functools.partial(owner_kernel, group), grid_spec=pltpu.Pr...  12.5 us
  transfers between devices with their start and end apart: 5, of which 4 were waited for; matrix products, arithmetic and copies ran while one was open for 4% of the time, Pallas kernels for 14%

profile of v2, /device:TPU:1, one launch (start us, length us, event | category | flops | bytes accessed | tf_op | source)
XLA Modules:
  0.0 351.8 jit_solution(6708210997896330402)
XLA Ops:
  7.2 0.8 pad_add_fusion
  8.0 0.1 copy.41
  8.1 20.8 %all_to_all.37 = s32[128,1,2]{2,1,0:T(1,128)S(1)} all-to-all(s32[128,1,2]{2,1,0:T(1,128)S(1)} %bitcast.25), channel_id=1, replica_groups=mesh['tm'=16,'rows'=8] {'tm','rows'}, dimensions={0} | all-to-all | bytes 2048 | tf_op jit(solution)/shard_map/all_to_all | solution.py:269
  28.9 0.8 slice_reduce_fusion
  29.7 3.7 %gather_fusion.1 = f32[128,64,128]{2,1,0:T(8,128)} fusion(f32[8,64,128]{2,1,0:T(8,128)} %param.19, s32[1024]{0:T(1024)S(1)} %pad_clamp_fusion), kind=kCustom, calls=%fused_computation.1 | custom fusion | bytes 8389120 | tf_op jit(solution)/shard_map/gather | solution.py:294
  33.4 5.6 %all-to-all-start.1 = ((f32[128,64,128]{2,1,0:T(8,128)}), f32[128,64,128]{2,1,0:T(8,128)}, u32[]{:S(2)}, u32[]{:S(2)}) async-start(f32[128,64,128]{2,1,0:T(8,128)} %gather_fusion.1), calls=%async_computation.1 | async-start | bytes 8388608 | tf_op jit(solution)/shard_map/all_to_all | solution.py:269
  39.0 4.9 %fusion.4 = f32[8,64,64]{2,0,1:T(8,128)S(1)} fusion(f32[64,64,64]{2,1,0:T(8,128)S(1)} %copy-done, f32[8,64]{1,0:T(8,128)S(1)} %copy-done.3), kind=kOutput, calls=%fused_computation.15 | convolution fusion | flops 25165824 | bytes 1181696 | tf_op jit(solution)/shard_map/pqr,sr->spq/dot_general | solution.py:297
  44.0 2.8 gather_fusion
  46.7 44.9 %all-to-all-done.1.items = f32[128,64,128]{2,1,0:T(8,128)} async-done(((f32[128,64,128]{2,1,0:T(8,128)}), f32[128,64,128]{2,1,0:T(8,128)}, u32[]{:S(2)}, u32[]{:S(2)}) %all-to-all-start.1) | async-done | bytes 4194336 | tf_op jit(solution)/shard_map/all_to_all | solution.py:269
  91.6 6.1 %all-to-all-start.2 = ((f32[128,64,128]{2,1,0:T(8,128)}), f32[128,64,128]{2,1,0:T(8,128)}, u32[]{:S(2)}, u32[]{:S(2)}) async-start(f32[128,64,128]{2,1,0:T(8,128)} %gather_fusion), calls=%async_computation.2 | async-start | bytes 8388608 | tf_op jit(solution)/shard_map/all_to_all | solution.py:269
  98.4 0.8 copy.42.cores
  99.2 19.9 %item_side.1 = (bf16[128,64,128]{2,1,0:T(8,128)(2,1)}, f32[128,64,128]{2,1,0:T(8,128)}, bf16[512,128,128]{2,1,0:T(8,128)(2,1)}, bf16[128,128,128]{2,1,0:T(8,128)(2,1)}) custom-call(s32[512]{0:T(512)} %slots_user.3, s32[512]{0:T(512)} %slots_item.3, s32[512]{0:T(512)} %steps.3, s32[1]{0:T(128)S(6)} %copy.50.count, f32[128,64,128]{2,1,0:T(8,128)} %all-to-all-done.1.items, ...), custom_call_target="tpu_custom_call" | custom-call | flops 20000000000 | bytes 50000000 | tf_op jit(solution)/shard_map/item_side/pallas_call | solution.py:121
  119.1 31.2 %all-to-all-done.2.users = f32[128,64,128]{2,1,0:T(8,128)} async-done(((f32[128,64,128]{2,1,0:T(8,128)}), f32[128,64,128]{2,1,0:T(8,128)}, u32[]{:S(2)}, u32[]{:S(2)}) %all-to-all-start.2) | async-done | bytes 4194336 | tf_op jit(solution)/shard_map/all_to_all | solution.py:269
  150.3 8.9 %user_grad.1 = f32[128,64,128]{2,1,0:T(8,128)} custom-call(f32[128,64,128]{2,1,0:T(8,128)} %all-to-all-done.2.users, bf16[128,64,128]{2,1,0:T(8,128)(2,1)} %get-tuple-element.23.gram, f32[128,64,128]{2,1,0:T(8,128)} %get-tuple-element.24.moved), custom_call_target="tpu_custom_call" | custom-call | flops 1000000000 | bytes 20000000 | tf_op jit(solution)/shard_map/user_grad/pallas_call | solution.py:154
  159.2 6.0 %all-to-all-start.3 = ((f32[128,64,128]{2,1,0:T(8,128)}), f32[128,64,128]{2,1,0:T(8,128)}, u32[]{:S(2)}, u32[]{:S(2)}) async-start(f32[128,64,128]{2,1,0:T(8,128)} %user_grad.1), calls=%async_computation.3 | async-start | bytes 8388608 | tf_op jit(solution)/shard_map/all_to_all | solution.py:269
  165.4 22.3 %tile_side.1 = (f32[128,64,128]{2,1,0:T(8,128)}, f32[8,64,64]{2,1,0:T(8,128)}) custom-call(s32[512]{0:T(512)} %slots_user.3, s32[512]{0:T(512)} %slots_item.3, s32[512]{0:T(512)} %steps.3, s32[1]{0:T(128)S(6)} %copy.50.count, f32[128,64,128]{2,1,0:T(8,128)} %all-to-all-done.2.users, bf16[128,128,128]{2,1,0:T(8,128)(2,1)} %get-tuple-element.26.right, ...), custom_call_target="tpu_custom_call" | custom-call | flops 30000001024 | bytes 50000000 | tf_op jit(solution)/shard_map/tile_side/pallas_call | solution.py:216
  187.6 1.1 reshape.28
  188.7 0.2 copy.44
  189.0 0.1 maximum_maximum_fusion
  189.1 28.7 %all-to-all-done.3.back = f32[128,64,128]{2,1,0:T(8,128)} async-done(((f32[128,64,128]{2,1,0:T(8,128)}), f32[128,64,128]{2,1,0:T(8,128)}, u32[]{:S(2)}, u32[]{:S(2)}) %all-to-all-start.3) | async-done | bytes 4194336 | tf_op jit(solution)/shard_map/all_to_all | solution.py:269
  217.8 0.1 copy.45
  218.0 16.3 %all_to_all.38 = f32[128,4,128]{2,1,0:T(4,128)S(1)} all-to-all(f32[128,4,128]{2,1,0:T(4,128)S(1)} %copy.45), channel_id=1, replica_groups=mesh['tm'=16,'rows'=8] {'tm','rows'}, dimensions={0} | all-to-all | bytes 524288 | tf_op jit(solution)/shard_map/all_to_all | solution.py:269
  234.2 5.5 %all-to-all-start.5 = ((f32[128,64,128]{2,1,0:T(8,128)}), f32[128,64,128]{2,1,0:T(8,128)}, u32[]{:S(2)}, u32[]{:S(2)}) async-start(f32[128,64,128]{2,1,0:T(8,128)} %get-tuple-element.33), calls=%async_computation.5 | async-start | bytes 8388608 | tf_op jit(solution)/shard_map/all_to_all | solution.py:269
  239.9 0.2 reshape.30
  240.2 0.9 convolution_multiply_fusion
  241.1 6.2 %owners.2 = f32[8,64,128]{2,1,0:T(8,128)} custom-call(s32[128]{0:T(128)} %get-tuple-element.39.held, f32[128,64,128]{2,1,0:T(8,128)} %all-to-all-done.3.back), custom_call_target="tpu_custom_call" | custom-call | tf_op jit(solution)/shard_map/owners/pallas_call | solution.py:254
  247.3 1.2 convolution_bitcast_fusion
  248.6 46.5 %psum.7 = f32[8,64]{1,0:T(8,128)S(1)} all-reduce(f32[8,64]{1,0:T(8,128)S(1)} %convolution_bitcast_fusion), channel_id=1, replica_groups=mesh['tm'=16,'rows'=8] {'rows'}, use_global_device_ids=true, to_apply=%region_0.1 | all-reduce | flops 512 | bytes 4096 | tf_op jit(solution)/shard_map/psum | solution.py:325
  295.1 0.6 broadcast_multiply_fusion
  295.7 39.9 %all-gather.2.cloned.1.call-done = f32[4096,64]{1,0:T(8,128)} async-done(((f32[32,64]{1,0:T(8,128)}), f32[4096,64]{1,0:T(8,128)}) %all-gather.2.cloned.1.call-update) | async-done | bytes 1048592 | tf_op jit(solution)/shard_map/all_gather | solution.py:323
  335.6 6.2 %owners.3 = f32[8,64,128]{2,1,0:T(8,128)} custom-call(s32[128]{0:T(128)} %get-tuple-element.36.held, f32[128,64,128]{2,1,0:T(8,128)} %all-to-all-done.5.back), custom_call_target="tpu_custom_call" | custom-call | tf_op jit(solution)/shard_map/owners/pallas_call | solution.py:254
  341.8 3.2 copy.51
  (20 shorter events, 0.4 us)
Async XLA Ops:
  7.2 31.8 %copy-start = (f32[64,64,64]{2,1,0:T(8,128)S(1)}, f32[64,64,64]{2,1,0:T(8,128)}, u32[]{:S(2)}) copy-start(f32[64,64,64]{2,1,0:T(8,128)} %param.21) | copy-start | bytes 3145732
  33.4 5.6 %copy-start.3 = (f32[8,64]{1,0:T(8,128)S(1)}, f32[8,64]{1,0:T(8,128)}, u32[]{:S(2)}) copy-start(f32[8,64]{1,0:T(8,128)} %param.20) | copy-start | bytes 6148
  33.4 10.6 %copy-start.1 = (f32[8,64,128]{2,1,0:T(8,128)S(1)}, f32[8,64,128]{2,1,0:T(8,128)}, u32[]{:S(2)}) copy-start(f32[8,64,128]{2,1,0:T(8,128)} %param.18) | copy-start | bytes 786436
  33.4 58.3 %all-to-all-start.1 = ((f32[128,64,128]{2,1,0:T(8,128)}), f32[128,64,128]{2,1,0:T(8,128)}, u32[]{:S(2)}, u32[]{:S(2)}) async-start(f32[128,64,128]{2,1,0:T(8,128)} %gather_fusion.1), calls=%async_computation.1 | async-start | bytes 8388608 | tf_op jit(solution)/shard_map/all_to_all | solution.py:269
  91.6 58.7 %all-to-all-start.2 = ((f32[128,64,128]{2,1,0:T(8,128)}), f32[128,64,128]{2,1,0:T(8,128)}, u32[]{:S(2)}, u32[]{:S(2)}) async-start(f32[128,64,128]{2,1,0:T(8,128)} %gather_fusion), calls=%async_computation.2 | async-start | bytes 8388608 | tf_op jit(solution)/shard_map/all_to_all | solution.py:269
  159.2 58.6 %all-to-all-start.3 = ((f32[128,64,128]{2,1,0:T(8,128)}), f32[128,64,128]{2,1,0:T(8,128)}, u32[]{:S(2)}, u32[]{:S(2)}) async-start(f32[128,64,128]{2,1,0:T(8,128)} %user_grad.1), calls=%async_computation.3 | async-start | bytes 8388608 | tf_op jit(solution)/shard_map/all_to_all | solution.py:269
  234.2 101.4 %all-to-all-start.5 = ((f32[128,64,128]{2,1,0:T(8,128)}), f32[128,64,128]{2,1,0:T(8,128)}, u32[]{:S(2)}, u32[]{:S(2)}) async-start(f32[128,64,128]{2,1,0:T(8,128)} %get-tuple-element.33), calls=%async_computation.5 | async-start | bytes 8388608 | tf_op jit(solution)/shard_map/all_to_all | solution.py:269
  239.7 7.6 %copy-start.2 = (f32[8,64,64]{2,1,0:T(8,128)S(1)}, f32[8,64,64]{2,1,0:T(8,128)}, u32[]{:S(2)}) copy-start(f32[8,64,64]{2,1,0:T(8,128)} %get-tuple-element.34) | copy-start | bytes 393220
  239.7 95.8 %all-gather.2.cloned.1.call-start = ((), (), s32[]{:S(2)}) async-start(), calls=%async_computation.6 | async-start | bytes 2113536 | tf_op jit(solution)/shard_map/all_gather | solution.py:323
Sparse Core Ops, SparseCore 0:
  244.3 91.2 all-gather.1

commit v3 on v2

--- a/solution.py
+++ b/solution.py
@@ -148,7 +148,7 @@
         grad[t] = out[t] - moved[t]
 
 
-def user_grad_call(users, gram, moved, group=16):
+def user_grad_call(users, gram, moved, group=64):
     held, rank, width = users.shape
     block = pl.BlockSpec((group, rank, width), lambda b: (b, 0, 0))
     return pl.pallas_call(
@@ -176,7 +176,7 @@
             h = [cat(split(y[:, :rank] + y[:, rank:]), 1) for y in h]
             for k, y, z in zip(ks, x, h):
                 left[k] = cat([-y[0], -y[1], z], 1)
-                grad[k] = jnp.zeros_like(grad[k])
+                grad[k, :rank] = jnp.zeros((rank, width), F32)
         in_groups(users.shape[0], PREP, prep)
         for k in range(cores.shape[0]):
             core_t[k] = cat(split(cores[k].T), 1)
@@ -200,7 +200,7 @@
             a = mul_t(cat(inner[t], 0), right[item[t]])
             dcore.append(a[:rank] + a[rank:])
         for t in span:
-            grad[item[t]] += grad_v[t]
+            grad[item[t], :rank] += grad_v[t]
             sums_hl[step[t]] += dcore[t]
 
     @pl.when(block == pl.num_programs(0) - 1)
@@ -210,7 +210,7 @@
             sums[k] = a[:, :rank] + a[:, rank:]
 
 
-def tile_call(slots_user, slots_item, steps, count, users, right, cores, values, mixed, group=32):
+def tile_call(slots_user, slots_item, steps, count, users, right, cores, values, mixed, extra, group=32):
     slots, width = values.shape[:2]
     held, rank = users.shape[:2]
     return pl.pallas_call(
@@ -221,47 +221,95 @@
             in_specs=[whole(users.shape), whole(right.shape), whole(cores.shape),
                       pl.BlockSpec((group, width, width), live_block(group)),
                       pl.BlockSpec((group, 2 * rank, width), live_block(group))],
-            out_specs=[whole((held, rank, width)), whole(cores.shape)],
+            out_specs=[whole((held, rank + extra, width)), whole(cores.shape)],
             scratch_shapes=[pltpu.VMEM((held, rank, 2 * width + 2 * rank), BF),
                             pltpu.VMEM((cores.shape[0], rank, 2 * rank), BF),
                             pltpu.VMEM((cores.shape[0], rank, 2 * rank), F32)],
         ),
-        out_shape=[jax.ShapeDtypeStruct((held, rank, width), F32),
+        out_shape=[jax.ShapeDtypeStruct((held, rank + extra, width), F32),
                    jax.ShapeDtypeStruct(cores.shape, F32)],
         compiler_params=params(),
         cost_estimate=pl.CostEstimate(flops=3 * 10**10, bytes_accessed=5 * 10**7, transcendentals=0),
         name="tile_side",
     )(slots_user, slots_item, steps, count, users, right, cores, values, mixed)
 
-def owner_kernel(group, held, back, out):
+def ask_kernel(group, held, table, out):
     block = pl.program_id(0)
-
-    @pl.when(block == 0)
-    def _():
-        out[...] = jnp.zeros_like(out)
-
     for t in range(group):
-        out[held[block * group + t]] += back[t]
-
-    @pl.when(block == pl.num_programs(0) - 1)
-    def _():
-        out[...] = out[...] * user_scale
-
-
-def owner_sum(held, back, blocks_own):
-    group = 16
-    total, rank, width = back.shape
+        out[t] = table[held[block * group + t]]
+
+
+def asked(held, table, group=16):
+    total = held.shape[0]
     return pl.pallas_call(
-        functools.partial(owner_kernel, group),
+        functools.partial(ask_kernel, group),
         grid_spec=pltpu.PrefetchScalarGridSpec(
             num_scalar_prefetch=1,
             grid=(total // group,),
-            in_specs=[pl.BlockSpec((group, rank, width), lambda b, *_: (b, 0, 0))],
-            out_specs=pl.BlockSpec((blocks_own, rank, width), lambda b, *_: (0, 0, 0)),
+            in_specs=[whole(table.shape)],
+            out_specs=pl.BlockSpec((group,) + table.shape[1:], lambda b, *_: (b, 0, 0)),
         ),
-        out_shape=jax.ShapeDtypeStruct((blocks_own, rank, width), F32),
-        compiler_params=pltpu.CompilerParams(dimension_semantics=("arbitrary",)),
-        name="owners",
+        out_shape=jax.ShapeDtypeStruct((total,) + table.shape[1:], F32),
+        compiler_params=params(),
+        cost_estimate=pl.CostEstimate(flops=0, bytes_accessed=10**7, transcendentals=0),
+        name="asked",
+    )(held, table)
+
+
+ADDERS = 4
+
+
+def owner_kernel(group, rank, scale, held, back, out, *rest):
+    block = pl.program_id(0)
+    core, adders = (rest[0], rest[1:]) if len(rest) > ADDERS else (None, rest)
+
+    @pl.when(block == 0)
+    def _():
+        for a in adders:
+            a[...] = jnp.zeros_like(a)
+
+    for t in range(0, group, ADDERS):
+        at = [held[block * group + t + k] for k in range(ADDERS)]
+        new = [adders[k][at[k]] + back[t + k, :rank] for k in range(ADDERS)]
+        for k in range(ADDERS):
+            adders[k][at[k]] = new[k]
+    if core is not None:
+        half = back.shape[2] // 2
+        new = [back[t, rank:] for t in range(group)]
+        new = [cat([x[:, :half], x[:, half:]], 0) for x in new]
+        size = new[0].shape[0]
+        for t in range(group):
+            core[t * size : (t + 1) * size] = new[t]
+
+    @pl.when(block == pl.num_programs(0) - 1)
+    def _():
+        total = adders[0][...]
+        for a in adders[1:]:
+            total = total + a[...]
+        out[...] = scale * total
+
+
+def owner_sum(held, back, blocks_own, rank, scale, group=16):
+    total, rows, width = back.shape
+    out_specs = [pl.BlockSpec((blocks_own, rank, width), lambda b, *_: (0, 0, 0))]
+    out_shape = [jax.ShapeDtypeStruct((blocks_own, rank, width), F32)]
+    if rows > rank:
+        part = 2 * (rows - rank)
+        out_specs.append(pl.BlockSpec((group * part, width // 2), lambda b, *_: (b, 0)))
+        out_shape.append(jax.ShapeDtypeStruct((total * part, width // 2), F32))
+    return pl.pallas_call(
+        functools.partial(owner_kernel, group, rank, scale),
+        grid_spec=pltpu.PrefetchScalarGridSpec(
+            num_scalar_prefetch=1,
+            grid=(total // group,),
+            in_specs=[pl.BlockSpec((group, rows, width), lambda b, *_: (b, 0, 0))],
+            out_specs=out_specs,
+            scratch_shapes=[pltpu.VMEM((blocks_own, rank, width), F32) for _ in range(ADDERS)],
+        ),
+        out_shape=out_shape,
+        compiler_params=params(),
+        cost_estimate=pl.CostEstimate(flops=10**7, bytes_accessed=10**7, transcendentals=0),
+        name="owner_sum",
     )(held, back)
 
 
@@ -289,11 +337,14 @@
     count_tm = lax.axis_size("tm")
     count_rows = lax.axis_size("rows")
     owners = count_tm * count_rows
+    part = rank * rank // owners
+    sum_rows = step_count * part // width
+    time_rows = step_count * rank // width
+    core_rows = part * rank // width
     asks = to_all(cat([users_ask, items_ask], 1))
     held_user, held_item = asks[:, 0], asks[:, 1]
-    found_item = item_factor.at[held_item].get(mode="promise_in_bounds")
-    items = to_all(found_item)
-    found_user = user_factor.at[held_user].get(mode="promise_in_bounds")
+    items = to_all(asked(held_item, item_factor))
+    found_user = asked(held_user, user_factor)
     step_cores = jnp.einsum("pqr,sr->spq", core, time_factor, precision=HIGH)
     found_user, items, step_cores = lax.optimization_barrier((found_user, items, step_cores))
     users = to_all(found_user)
@@ -304,27 +355,30 @@
     users, slot_left = lax.optimization_barrier((users, slot_left))
     back_left = to_all(slot_left)
     slot_right, step_sums = tile_call(
-        tile_users, tile_items, tile_steps, tile_count, users, right, step_cores, tile_values, mixed
+        tile_users, tile_items, tile_steps, tile_count, users, right, step_cores, tile_values, mixed, core_rows
     )
-    part = rank * rank // owners
-    parts = step_sums.reshape(step_count, owners, part).transpose(1, 0, 2)
+    parts = step_sums.reshape(step_count, owners, part).transpose(1, 0, 2).reshape(owners, sum_rows, width)
     row = lax.dynamic_slice_in_dim(time_factor, lax.axis_index("rows"), 1, 0)
-    row = jnp.broadcast_to(jnp.pad(row, ((0, 0), (0, width - rank)))[None], (owners, 1, width))
-    blank = jnp.zeros((owners, 1, width), F32)
-    sent = cat([parts.reshape(owners, -1, width), row, blank], 1)
+    row = jnp.pad(row, ((0, 0), (0, width - rank)))
+    own_time = jnp.einsum("spq,pqr->sr", step_sums, core, precision=HIGH).reshape(time_rows, width)
+    blank = jnp.zeros((-(sum_rows + 1 + time_rows) % 8, width), F32)
+    shared = cat([row, own_time, blank], 0)
+    sent = cat([parts, jnp.broadcast_to(shared[None], (owners,) + shared.shape)], 1)
     sent, back_left = lax.optimization_barrier((sent, back_left))
     got = to_all(sent)
-    got, slot_right, step_sums = lax.optimization_barrier((got, slot_right, step_sums))
+    some = got[:, :sum_rows].reshape(count_tm, count_rows, step_count, part)
+    some = jnp.sum(some, axis=1).reshape(count_tm * step_count, part)
+    every_time = got[:, sum_rows, :rank]
+    own = core_scale * jnp.einsum("sk,sr->kr", some, every_time, precision=HIGH)
+    own = cat([own[:core_rows], own[core_rows:]], 1)
+    slot_right = slot_right.at[:, rank:].set(jnp.broadcast_to(own[None], (owners, core_rows, width)))
     back_right = to_all(slot_right)
-    some = got[:, : step_count * part // width].reshape(count_tm, count_rows, step_count, part)
-    some = jnp.sum(some, axis=1).reshape(count_tm * step_count, part)
-    every_time = got[:, step_count * part // width, :rank]
-    own = core_scale * jnp.einsum("sk,sr->kr", some, every_time, precision=HIGH)
-    grad_core = lax.all_gather(own, AXES, axis=0, tiled=True).reshape(rank, rank, rank)
-    own_time = jnp.einsum("spq,pqr->sr", step_sums, core, precision=HIGH)
-    grad_time = time_scale * lax.psum(own_time, "rows")
-    grad_users = owner_sum(held_user, back_left, blocks_own)
-    grad_items = owner_sum(held_item, back_right, blocks_own)
+    first = lax.axis_index("tm") * count_rows
+    terms = lax.dynamic_slice_in_dim(got, first, count_rows, 0)[:, sum_rows + 1 : sum_rows + 1 + time_rows]
+    grad_time = time_scale * jnp.sum(terms, axis=0).reshape(step_count, rank)
+    (grad_users,) = owner_sum(held_user, back_left, blocks_own, rank, user_scale)
+    grad_items, grad_core = owner_sum(held_item, back_right, blocks_own, rank, user_scale)
+    grad_core = grad_core.reshape(rank, rank, rank)
     return (grad_users, grad_items, grad_time, grad_core)
 
 

time: 353 us -> 309 us (0.88)
  Pallas kernels: 63.6 us -> 113 us
  blocking collectives: 83.6 us -> 39.7 us
  waiting for transfers between devices: 145 us -> 117 us
  between operations: 14.8 us -> 1.42 us
  local copies, waits for them, and re-layouts: 12.4 us -> 5.29 us
    psum x1 -> x0, blocking collectives: 46.5 us -> none  [shards(): grad_time = time_scale * lax.psum(own_time, 'rows')]
    all_gather x1 -> x0, waiting for transfers between devices: 39.9 us -> none  [shards(): lax.all_gather(own, AXES, axis=0, tiled=True).reshape(rank, rank, rank)]
    pallas_call x1, Pallas kernels: 22.3 us -> 42.9 us  [tile_call(): pl.pallas_call(functools.partial(tile_kernel, group), grid_spec=pltpu.Pre...]
    pallas_call x1, Pallas kernels: 19.9 us -> 40.1 us  [item_call(): pl.pallas_call(functools.partial(item_kernel, group), grid_spec=pltpu.Pre...]
    all_to_all x4, waiting for transfers between devices: 105 us -> 117 us  [to_all(): return lax.all_to_all(x, AXES, split_axis=0, concat_axis=0, tiled=True)]
    pallas_call x2 -> x4, Pallas kernels: 12.5 us -> 24 us  [the longest x2 13.6 us: owner_sum(): pl.pallas_call(functools.partial(owner_kernel, group, rank, scale), grid_...]
    gather x2 -> x0, local copies, waits for them, and re-layouts: 6.46 us -> none  [the longest x1 3.7 us: shards(): found_item = item_factor.at[held_item].get(mode='promise_in_bounds')]
  transfers between devices with their start and end apart: 5 -> 4, of which waited for: 4 -> 4; matrix products, arithmetic and copies ran while one was open for 4% -> 3% of each run, Pallas kernels for 14% -> 31%
where the time goes in v3:
time: 309 us
  waiting for transfers between devices  117 us (38%)
  Pallas kernels  113 us (37%)
  blocking collectives  39.7 us (13%)
  starting transfers between devices  23.4 us (8%)
  matrix products  7.38 us (2%)
  local copies, waits for them, and re-layouts  5.29 us (2%)
    all_to_all x4, waiting for transfers between devices, to_all(): return lax.all_to_all(x, AXES, split_axis=0, concat_axis=0, tiled=True)  117 us
    pallas_call x1, Pallas kernels, tile_call(): pl.pallas_call(functools.partial(tile_kernel, group), grid_spec=pltpu.Pre...  42.9 us
    pallas_call x1, Pallas kernels, item_call(): pl.pallas_call(functools.partial(item_kernel, group), grid_spec=pltpu.Pre...  40.1 us
    all_to_all x2, blocking collectives, to_all(): return lax.all_to_all(x, AXES, split_axis=0, concat_axis=0, tiled=True)  39.7 us
    all_to_all x4, starting transfers between devices, to_all(): return lax.all_to_all(x, AXES, split_axis=0, concat_axis=0, tiled=True)  23.4 us
    pallas_call x2, Pallas kernels, owner_sum(): pl.pallas_call(functools.partial(owner_kernel, group, rank, scale), grid_...  13.6 us
    pallas_call x2, Pallas kernels, asked(): pl.pallas_call(functools.partial(ask_kernel, group), grid_spec=pltpu.Pref...  10.4 us
  transfers between devices with their start and end apart: 4, of which 4 were waited for; matrix products, arithmetic and copies ran while one was open for 3% of the time, Pallas kernels for 31%

profile of v3, /device:TPU:1, one launch (start us, length us, event | category | flops | bytes accessed | tf_op | source)
XLA Modules:
  0.0 308.5 jit_solution(14002598022485420626)
XLA Ops:
  0.6 0.8 pad_add_fusion
  1.5 0.1 copy.49
  1.6 20.8 %all_to_all.37 = s32[128,1,2]{2,1,0:T(1,128)S(1)} all-to-all(s32[128,1,2]{2,1,0:T(1,128)S(1)} %bitcast.21), channel_id=1, replica_groups=mesh['tm'=16,'rows'=8] {'tm','rows'}, dimensions={0} | all-to-all | bytes 2048 | tf_op jit(solution)/shard_map/all_to_all | solution.py:317
  22.4 0.7 slice_reduce_fusion
  23.1 5.2 %asked.3 = f32[128,64,128]{2,1,0:T(8,128)} custom-call(s32[128]{0:T(128)} %get-tuple-element.46.held, f32[8,64,128]{2,1,0:T(8,128)} %table.3), custom_call_target="tpu_custom_call" | custom-call | bytes 10000000 | tf_op jit(solution)/shard_map/asked/pallas_call | solution.py:244
  28.3 5.6 %all-to-all-start.1 = ((f32[128,64,128]{2,1,0:T(8,128)}), f32[128,64,128]{2,1,0:T(8,128)}, u32[]{:S(2)}, u32[]{:S(2)}) async-start(f32[128,64,128]{2,1,0:T(8,128)} %asked.3), calls=%async_computation.1 | async-start | bytes 8388608 | tf_op jit(solution)/shard_map/all_to_all | solution.py:317
  33.9 4.9 %fusion.3 = f32[8,64,64]{2,0,1:T(8,128)S(1)} fusion(f32[64,64,64]{2,1,0:T(8,128)S(1)} %copy-done, f32[8,64]{1,0:T(8,128)S(1)} %copy-done.1), kind=kOutput, calls=%fused_computation.13 | convolution fusion | flops 25165824 | bytes 1181696 | tf_op jit(solution)/shard_map/pqr,sr->spq/dot_general | solution.py:348
  38.9 5.2 %asked.2 = f32[128,64,128]{2,1,0:T(8,128)} custom-call(s32[128]{0:T(128)} %get-tuple-element.47.held, f32[8,64,128]{2,1,0:T(8,128)} %table.2), custom_call_target="tpu_custom_call" | custom-call | bytes 10000000 | tf_op jit(solution)/shard_map/asked/pallas_call | solution.py:244
  44.1 42.5 %all-to-all-done.1.items = f32[128,64,128]{2,1,0:T(8,128)} async-done(((f32[128,64,128]{2,1,0:T(8,128)}), f32[128,64,128]{2,1,0:T(8,128)}, u32[]{:S(2)}, u32[]{:S(2)}) %all-to-all-start.1) | async-done | bytes 4194336 | tf_op jit(solution)/shard_map/all_to_all | solution.py:317
  86.6 6.1 %all-to-all-start.2 = ((f32[128,64,128]{2,1,0:T(8,128)}), f32[128,64,128]{2,1,0:T(8,128)}, u32[]{:S(2)}, u32[]{:S(2)}) async-start(f32[128,64,128]{2,1,0:T(8,128)} %asked.2), calls=%async_computation.2 | async-start | bytes 8388608 | tf_op jit(solution)/shard_map/all_to_all | solution.py:317
  93.4 0.8 copy.50.cores
  94.1 40.1 %item_side.1 = (bf16[128,64,128]{2,1,0:T(8,128)(2,1)}, f32[128,64,128]{2,1,0:T(8,128)}, bf16[512,128,128]{2,1,0:T(8,128)(2,1)}, bf16[128,128,128]{2,1,0:T(8,128)(2,1)}) custom-call(s32[512]{0:T(512)} %slots_user.3, s32[512]{0:T(512)} %slots_item.3, s32[512]{0:T(512)} %steps.3, s32[1]{0:T(128)S(6)} %copy.60.count, f32[128,64,128]{2,1,0:T(8,128)} %all-to-all-done.1.items, ...), custom_call_target="tpu_custom_call" | custom-call | flops 20000000000 | bytes 50000000 | tf_op jit(solution)/shard_map/item_side/pallas_call | solution.py:121
  134.2 11.0 %all-to-all-done.2.users = f32[128,64,128]{2,1,0:T(8,128)} async-done(((f32[128,64,128]{2,1,0:T(8,128)}), f32[128,64,128]{2,1,0:T(8,128)}, u32[]{:S(2)}, u32[]{:S(2)}) %all-to-all-start.2) | async-done | bytes 4194336 | tf_op jit(solution)/shard_map/all_to_all | solution.py:317
  145.3 6.2 %user_grad.1 = f32[128,64,128]{2,1,0:T(8,128)} custom-call(f32[128,64,128]{2,1,0:T(8,128)} %all-to-all-done.2.users, bf16[128,64,128]{2,1,0:T(8,128)(2,1)} %get-tuple-element.34.gram, f32[128,64,128]{2,1,0:T(8,128)} %get-tuple-element.35.moved), custom_call_target="tpu_custom_call" | custom-call | flops 1000000000 | bytes 20000000 | tf_op jit(solution)/shard_map/user_grad/pallas_call | solution.py:154
  151.4 6.0 %all-to-all-start.3 = ((f32[128,64,128]{2,1,0:T(8,128)}), f32[128,64,128]{2,1,0:T(8,128)}, u32[]{:S(2)}, u32[]{:S(2)}) async-start(f32[128,64,128]{2,1,0:T(8,128)} %user_grad.1), calls=%async_computation.3 | async-start | bytes 8388608 | tf_op jit(solution)/shard_map/all_to_all | solution.py:317
  157.5 42.9 %tile_side.1 = (f32[128,80,128]{2,1,0:T(8,128)}, f32[8,64,64]{2,1,0:T(8,128)}) custom-call(s32[512]{0:T(512)} %slots_user.3, s32[512]{0:T(512)} %slots_item.3, s32[512]{0:T(512)} %steps.3, s32[1]{0:T(128)S(6)} %copy.60.count, f32[128,64,128]{2,1,0:T(8,128)} %all-to-all-done.2.users, bf16[128,128,128]{2,1,0:T(8,128)(2,1)} %get-tuple-element.37.right, ...), custom_call_target="tpu_custom_call" | custom-call | flops 30000001024 | bytes 50000000 | tf_op jit(solution)/shard_map/tile_side/pallas_call | solution.py:216
  200.5 1.1 reshape.62
  201.6 2.2 convolution_bitcast_fusion
  203.8 0.1 reshape.64
  203.8 0.2 copy.52
  204.0 0.1 copy.54
  204.3 0.1 pad_maximum_fusion
  204.4 5.6 %all-to-all-done.3.back = f32[128,64,128]{2,1,0:T(8,128)} async-done(((f32[128,64,128]{2,1,0:T(8,128)}), f32[128,64,128]{2,1,0:T(8,128)}, u32[]{:S(2)}, u32[]{:S(2)}) %all-to-all-start.3) | async-done | bytes 4194336 | tf_op jit(solution)/shard_map/all_to_all | solution.py:317
  210.0 18.9 %all_to_all.38 = f32[128,8,128]{2,1,0:T(8,128)S(1)} all-to-all(f32[128,8,128]{2,1,0:T(8,128)S(1)} %pad_maximum_fusion), channel_id=1, replica_groups=mesh['tm'=16,'rows'=8] {'tm','rows'}, dimensions={0} | all-to-all | bytes 1048576 | tf_op jit(solution)/shard_map/all_to_all | solution.py:317
  228.9 0.2 reshape.65
  229.3 0.3 convolution_multiply_fusion
  229.6 1.1 broadcast_dynamic-update-slice_fusion
  230.7 5.6 %all-to-all-start.5 = ((f32[128,80,128]{2,1,0:T(8,128)}), f32[128,80,128]{2,1,0:T(8,128)}, u32[]{:S(2)}, u32[]{:S(2)}) async-start(f32[128,80,128]{2,1,0:T(8,128)} %broadcast_dynamic-update-slice_fusion), calls=%async_computation.5 | async-start | bytes 10485760 | tf_op jit(solution)/shard_map/all_to_all | solution.py:317
  236.4 6.2 %owner_sum.2 = f32[8,64,128]{2,1,0:T(8,128)} custom-call(s32[128]{0:T(128)} %get-tuple-element.47.held, f32[128,64,128]{2,1,0:T(8,128)} %all-to-all-done.3.back), custom_call_target="tpu_custom_call" | custom-call | flops 10000000 | bytes 10000000 | tf_op jit(solution)/shard_map/owner_sum/pallas_call | solution.py:300
  242.6 0.7 mul.23
  243.2 57.8 %all-to-all-done.5.back = f32[128,80,128]{2,1,0:T(8,128)} async-done(((f32[128,80,128]{2,1,0:T(8,128)}), f32[128,80,128]{2,1,0:T(8,128)}, u32[]{:S(2)}, u32[]{:S(2)}) %all-to-all-start.5) | async-done | bytes 5242912 | tf_op jit(solution)/shard_map/all_to_all | solution.py:317
  301.1 7.4 %owner_sum.3 = (f32[8,64,128]{2,1,0:T(8,128)}, f32[4096,64]{1,0:T(8,128)}) custom-call(s32[128]{0:T(128)} %get-tuple-element.46.held, f32[128,80,128]{2,1,0:T(8,128)} %all-to-all-done.5.back), custom_call_target="tpu_custom_call" | custom-call | flops 10000000 | bytes 10000000 | tf_op jit(solution)/shard_map/owner_sum/pallas_call | solution.py:300
  (15 shorter events, 0.4 us)
Async XLA Ops:
  0.6 33.3 %copy-start = (f32[64,64,64]{2,1,0:T(8,128)S(1)}, f32[64,64,64]{2,1,0:T(8,128)}, u32[]{:S(2)}) copy-start(f32[64,64,64]{2,1,0:T(8,128)} %param.23) | copy-start | bytes 3145732
  28.3 5.6 %copy-start.1 = (f32[8,64]{1,0:T(8,128)S(1)}, f32[8,64]{1,0:T(8,128)}, u32[]{:S(2)}) copy-start(f32[8,64]{1,0:T(8,128)} %param.22) | copy-start | bytes 6148
  28.3 58.2 %all-to-all-start.1 = ((f32[128,64,128]{2,1,0:T(8,128)}), f32[128,64,128]{2,1,0:T(8,128)}, u32[]{:S(2)}, u32[]{:S(2)}) async-start(f32[128,64,128]{2,1,0:T(8,128)} %asked.3), calls=%async_computation.1 | async-start | bytes 8388608 | tf_op jit(solution)/shard_map/all_to_all | solution.py:317
  86.6 58.7 %all-to-all-start.2 = ((f32[128,64,128]{2,1,0:T(8,128)}), f32[128,64,128]{2,1,0:T(8,128)}, u32[]{:S(2)}, u32[]{:S(2)}) async-start(f32[128,64,128]{2,1,0:T(8,128)} %asked.2), calls=%async_computation.2 | async-start | bytes 8388608 | tf_op jit(solution)/shard_map/all_to_all | solution.py:317
  151.4 58.6 %all-to-all-start.3 = ((f32[128,64,128]{2,1,0:T(8,128)}), f32[128,64,128]{2,1,0:T(8,128)}, u32[]{:S(2)}, u32[]{:S(2)}) async-start(f32[128,64,128]{2,1,0:T(8,128)} %user_grad.1), calls=%async_computation.3 | async-start | bytes 8388608 | tf_op jit(solution)/shard_map/all_to_all | solution.py:317
  230.7 70.3 %all-to-all-start.5 = ((f32[128,80,128]{2,1,0:T(8,128)}), f32[128,80,128]{2,1,0:T(8,128)}, u32[]{:S(2)}, u32[]{:S(2)}) async-start(f32[128,80,128]{2,1,0:T(8,128)} %broadcast_dynamic-update-slice_fusion), calls=%async_computation.5 | async-start | bytes 10485760 | tf_op jit(solution)/shard_map/all_to_all | solution.py:317

commit v4 on v3

--- a/solution.py
+++ b/solution.py
@@ -141,23 +141,51 @@
     )(slots_user, slots_item, steps, count, items, cores, values)
 
 
-def user_grad_kernel(group, users, gram, moved, grad):
-    span = range(group)
-    out = [mul(twice(gram[t]), quad(*split(users[t]))) for t in span]
-    for t in span:
-        grad[t] = out[t] - moved[t]
-
-
-def user_grad_call(users, gram, moved, group=64):
-    held, rank, width = users.shape
-    block = pl.BlockSpec((group, rank, width), lambda b: (b, 0, 0))
-    return pl.pallas_call(
-        functools.partial(user_grad_kernel, group),
-        grid=(held // group,),
-        in_specs=[block, pl.BlockSpec((group, rank, 2 * rank), lambda b: (b, 0, 0)), block],
-        out_specs=block,
+CHUNKS = 8
+
+
+def user_grad_kernel(users, gram, moved, grad, users_v, gram_v, moved_v, grad_v, sems):
+    size = users_v.shape[0] // CHUNKS
+
+    def copies(c):
+        at = pl.ds(c * size, size)
+        pieces = ((users, users_v), (gram, gram_v), (moved, moved_v))
+        return [pltpu.make_async_copy(a.at[at], b.at[at], sems.at[k, c]) for k, (a, b) in enumerate(pieces)]
+
+    def back(c):
+        at = pl.ds(c * size, size)
+        return pltpu.make_async_copy(grad_v.at[at], grad.at[at], sems.at[3, c])
+
+    for c in range(CHUNKS):
+        for copy in copies(c):
+            copy.start()
+    for c in range(CHUNKS):
+        for copy in copies(c):
+            copy.wait()
+        span = range(c * size, (c + 1) * size)
+        out = [mul(twice(gram_v[t]), quad(*split(users_v[t]))) for t in span]
+        for t, x in zip(span, out):
+            grad_v[t] = x - moved_v[t]
+        back(c).start()
+    for c in range(CHUNKS):
+        back(c).wait()
+
+
+def user_grad_call(users, gram, moved):
+    any_space = pl.BlockSpec(memory_space=pl.ANY)
+    return pl.pallas_call(
+        user_grad_kernel,
+        in_specs=[any_space] * 3,
+        out_specs=any_space,
         out_shape=jax.ShapeDtypeStruct(users.shape, F32),
-        compiler_params=params(),
+        scratch_shapes=[
+            pltpu.VMEM(users.shape, F32),
+            pltpu.VMEM(gram.shape, BF),
+            pltpu.VMEM(users.shape, F32),
+            pltpu.VMEM(users.shape, F32),
+            pltpu.SemaphoreType.DMA((4, CHUNKS)),
+        ],
+        compiler_params=pltpu.CompilerParams(vmem_limit_bytes=60 * 2**20),
         cost_estimate=pl.CostEstimate(flops=10**9, bytes_accessed=2 * 10**7, transcendentals=0),
         name="user_grad",
     )(users, gram, moved)
@@ -233,24 +261,32 @@
         name="tile_side",
     )(slots_user, slots_item, steps, count, users, right, cores, values, mixed)
 
-def ask_kernel(group, held, table, out):
-    block = pl.program_id(0)
-    for t in range(group):
-        out[t] = table[held[block * group + t]]
-
-
-def asked(held, table, group=16):
-    total = held.shape[0]
-    return pl.pallas_call(
-        functools.partial(ask_kernel, group),
-        grid_spec=pltpu.PrefetchScalarGridSpec(
-            num_scalar_prefetch=1,
-            grid=(total // group,),
-            in_specs=[whole(table.shape)],
-            out_specs=pl.BlockSpec((group,) + table.shape[1:], lambda b, *_: (b, 0, 0)),
-        ),
-        out_shape=jax.ShapeDtypeStruct((total,) + table.shape[1:], F32),
-        compiler_params=params(),
+def ask_kernel(held, table, out, buffer, sems):
+    size = buffer.shape[0] // CHUNKS
+
+    def send(c):
+        at = pl.ds(c * size, size)
+        return pltpu.make_async_copy(buffer.at[at], out.at[at], sems.at[c])
+
+    for c in range(CHUNKS):
+        for t in range(c * size, (c + 1) * size, 4):
+            new = [table[held[t + k]] for k in range(4)]
+            for k in range(4):
+                buffer[t + k] = new[k]
+        send(c).start()
+    for c in range(CHUNKS):
+        send(c).wait()
+
+
+def asked(held, table):
+    shape = (held.shape[0],) + table.shape[1:]
+    return pl.pallas_call(
+        ask_kernel,
+        in_specs=[pl.BlockSpec(memory_space=pltpu.SMEM), pl.BlockSpec(memory_space=pltpu.VMEM)],
+        out_specs=pl.BlockSpec(memory_space=pl.ANY),
+        out_shape=jax.ShapeDtypeStruct(shape, F32),
+        scratch_shapes=[pltpu.VMEM(shape, F32), pltpu.SemaphoreType.DMA((CHUNKS,))],
+        compiler_params=pltpu.CompilerParams(vmem_limit_bytes=60 * 2**20),
         cost_estimate=pl.CostEstimate(flops=0, bytes_accessed=10**7, transcendentals=0),
         name="asked",
     )(held, table)
@@ -259,58 +295,76 @@
 ADDERS = 4
 
 
-def owner_kernel(group, rank, scale, held, back, out, *rest):
-    block = pl.program_id(0)
-    core, adders = (rest[0], rest[1:]) if len(rest) > ADDERS else (None, rest)
-
-    @pl.when(block == 0)
-    def _():
-        for a in adders:
-            a[...] = jnp.zeros_like(a)
-
-    for t in range(0, group, ADDERS):
-        at = [held[block * group + t + k] for k in range(ADDERS)]
-        new = [adders[k][at[k]] + back[t + k, :rank] for k in range(ADDERS)]
-        for k in range(ADDERS):
-            adders[k][at[k]] = new[k]
-    if core is not None:
-        half = back.shape[2] // 2
-        new = [back[t, rank:] for t in range(group)]
-        new = [cat([x[:, :half], x[:, half:]], 0) for x in new]
-        size = new[0].shape[0]
-        for t in range(group):
-            core[t * size : (t + 1) * size] = new[t]
-
-    @pl.when(block == pl.num_programs(0) - 1)
-    def _():
-        total = adders[0][...]
-        for a in adders[1:]:
-            total = total + a[...]
-        out[...] = scale * total
-
-
-def owner_sum(held, back, blocks_own, rank, scale, group=16):
+def owner_kernel(rank, scale, held, back, out, *rest):
+    adders, (back_v, sems) = rest[:ADDERS], rest[ADDERS:]
+    size = back_v.shape[0] // CHUNKS
+
+    def fetch(c):
+        at = pl.ds(c * size, size)
+        return pltpu.make_async_copy(back.at[at, pl.ds(0, rank)], back_v.at[at], sems.at[c])
+
+    for c in range(CHUNKS):
+        fetch(c).start()
+    for a in adders:
+        a[...] = jnp.zeros_like(a)
+    for c in range(CHUNKS):
+        fetch(c).wait()
+        for t in range(c * size, (c + 1) * size, ADDERS):
+            at = [held[t + k] for k in range(ADDERS)]
+            new = [adders[k][at[k]] + back_v[t + k] for k in range(ADDERS)]
+            for k in range(ADDERS):
+                adders[k][at[k]] = new[k]
+    total = adders[0][...]
+    for a in adders[1:]:
+        total = total + a[...]
+    out[...] = scale * total
+
+
+def owner_sum(held, back, blocks_own, rank, scale):
     total, rows, width = back.shape
-    out_specs = [pl.BlockSpec((blocks_own, rank, width), lambda b, *_: (0, 0, 0))]
-    out_shape = [jax.ShapeDtypeStruct((blocks_own, rank, width), F32)]
-    if rows > rank:
-        part = 2 * (rows - rank)
-        out_specs.append(pl.BlockSpec((group * part, width // 2), lambda b, *_: (b, 0)))
-        out_shape.append(jax.ShapeDtypeStruct((total * part, width // 2), F32))
-    return pl.pallas_call(
-        functools.partial(owner_kernel, group, rank, scale),
-        grid_spec=pltpu.PrefetchScalarGridSpec(
-            num_scalar_prefetch=1,
-            grid=(total // group,),
-            in_specs=[pl.BlockSpec((group, rows, width), lambda b, *_: (b, 0, 0))],
-            out_specs=out_specs,
-            scratch_shapes=[pltpu.VMEM((blocks_own, rank, width), F32) for _ in range(ADDERS)],
-        ),
-        out_shape=out_shape,
-        compiler_params=params(),
+    return pl.pallas_call(
+        functools.partial(owner_kernel, rank, scale),
+        in_specs=[pl.BlockSpec(memory_space=pltpu.SMEM), pl.BlockSpec(memory_space=pl.ANY)],
+        out_specs=pl.BlockSpec(memory_space=pltpu.VMEM),
+        out_shape=jax.ShapeDtypeStruct((blocks_own, rank, width), F32),
+        scratch_shapes=[pltpu.VMEM((blocks_own, rank, width), F32) for _ in range(ADDERS)]
+        + [pltpu.VMEM((total, rank, width), F32), pltpu.SemaphoreType.DMA((CHUNKS,))],
+        compiler_params=pltpu.CompilerParams(vmem_limit_bytes=60 * 2**20),
         cost_estimate=pl.CostEstimate(flops=10**7, bytes_accessed=10**7, transcendentals=0),
         name="owner_sum",
     )(held, back)
+
+
+def core_kernel(odd, mine, other, core):
+    half = mine.shape[2] // 2
+    rows = 2 * mine.shape[1]
+
+    def step(ks):
+        a = [mine[k] for k in ks]
+        b = [other[k] for k in ks]
+        new = []
+        for x, y in zip(a, b):
+            new.append((jnp.where(odd[0] == 0, x, y), jnp.where(odd[0] == 0, y, x)))
+        new = [[cat([x[:, :half], x[:, half:]], 0) for x in pair] for pair in new]
+        for k, (x, y) in zip(ks, new):
+            core[k, :rows] = x
+            core[k, rows:] = y
+
+    for g in range(0, mine.shape[0], PREP):
+        step(range(g, g + PREP))
+
+
+def core_unpack(odd, mine, other):
+    owners, rows, width = mine.shape
+    return pl.pallas_call(
+        core_kernel,
+        in_specs=[pl.BlockSpec(memory_space=pltpu.SMEM)] + [pl.BlockSpec(memory_space=pltpu.VMEM)] * 2,
+        out_specs=pl.BlockSpec(memory_space=pltpu.VMEM),
+        out_shape=jax.ShapeDtypeStruct((owners, 4 * rows, width // 2), F32),
+        compiler_params=pltpu.CompilerParams(vmem_limit_bytes=60 * 2**20),
+        cost_estimate=pl.CostEstimate(flops=10**6, bytes_accessed=3 * 10**6, transcendentals=0),
+        name="core_unpack",
+    )(odd, mine, other)
 
 
 def to_all(x):
@@ -340,7 +394,7 @@
     part = rank * rank // owners
     sum_rows = step_count * part // width
     time_rows = step_count * rank // width
-    core_rows = part * rank // width
+    core_rows = part * rank // width // 2
     asks = to_all(cat([users_ask, items_ask], 1))
     held_user, held_item = asks[:, 0], asks[:, 1]
     items = to_all(asked(held_item, item_factor))
@@ -370,15 +424,20 @@
     some = jnp.sum(some, axis=1).reshape(count_tm * step_count, part)
     every_time = got[:, sum_rows, :rank]
     own = core_scale * jnp.einsum("sk,sr->kr", some, every_time, precision=HIGH)
-    own = cat([own[:core_rows], own[core_rows:]], 1)
-    slot_right = slot_right.at[:, rank:].set(jnp.broadcast_to(own[None], (owners, core_rows, width)))
+    own = own.reshape(2, 2, core_rows, rank).transpose(0, 2, 1, 3).reshape(1, 2, core_rows, width)
+    own = jnp.broadcast_to(own, (owners // 2, 2, core_rows, width)).reshape(owners, core_rows, width)
+    slot_right = slot_right.at[:, rank:].set(own)
     back_right = to_all(slot_right)
     first = lax.axis_index("tm") * count_rows
     terms = lax.dynamic_slice_in_dim(got, first, count_rows, 0)[:, sum_rows + 1 : sum_rows + 1 + time_rows]
     grad_time = time_scale * jnp.sum(terms, axis=0).reshape(step_count, rank)
-    (grad_users,) = owner_sum(held_user, back_left, blocks_own, rank, user_scale)
-    grad_items, grad_core = owner_sum(held_item, back_right, blocks_own, rank, user_scale)
-    grad_core = grad_core.reshape(rank, rank, rank)
+    grad_users = owner_sum(held_user, back_left, blocks_own, rank, user_scale)
+    back_right, grad_users, grad_time = lax.optimization_barrier((back_right, grad_users, grad_time))
+    mine = back_right[:, rank:]
+    other = lax.ppermute(mine, "rows", [(r, r ^ 1) for r in range(count_rows)])
+    grad_items = owner_sum(held_item, back_right, blocks_own, rank, user_scale)
+    odd = (lax.axis_index("rows") % 2).astype(jnp.int32).reshape(1)
+    grad_core = core_unpack(odd, mine, other).reshape(rank, rank, rank)
     return (grad_users, grad_items, grad_time, grad_core)
 
 

time: 309 us -> 303 us (0.981)
  Pallas kernels: 113 us -> 65 us
  waiting for transfers between devices: 117 us -> 156 us
    all_to_all x4, waiting for transfers between devices: 117 us -> 156 us  [to_all(): return lax.all_to_all(x, AXES, split_axis=0, concat_axis=0, tiled=True)]
    pallas_call x1, Pallas kernels: 42.9 us -> 22.5 us  [tile_call(): pl.pallas_call(functools.partial(tile_kernel, group), grid_spec=pltpu.Pre...]
    pallas_call x1, Pallas kernels: 40.1 us -> 20 us  [item_call(): pl.pallas_call(functools.partial(item_kernel, group), grid_spec=pltpu.Pre...]
    pallas_call x5 -> x6, Pallas kernels: 30.2 us -> 22.6 us  [the longest x2 7.41 us: owner_sum(): pl.pallas_call(functools.partial(owner_kernel, rank, scale), in_specs=[pl...]
  transfers between devices with their start and end apart: 4 -> 5, of which waited for: 4 -> 4; matrix products, arithmetic and copies ran while one was open for 3% -> 3% of each run, Pallas kernels for 31% -> 17%
where the time goes in v4:
time: 303 us; the launch traced here: 302 us
  waiting for transfers between devices  156 us (51%)
  Pallas kernels  65 us (21%)
  blocking collectives  39.7 us (13%)
  starting transfers between devices  24.4 us (8%)
  matrix products  7.38 us (2%)
  local copies, waits for them, and re-layouts  7.03 us (2%)
    all_to_all x4, waiting for transfers between devices, to_all(): return lax.all_to_all(x, AXES, split_axis=0, concat_axis=0, tiled=True)  156 us
    all_to_all x2, blocking collectives, to_all(): return lax.all_to_all(x, AXES, split_axis=0, concat_axis=0, tiled=True)  39.7 us
    all_to_all x4, starting transfers between devices, to_all(): return lax.all_to_all(x, AXES, split_axis=0, concat_axis=0, tiled=True)  23.3 us
    pallas_call x1, Pallas kernels, tile_call(): pl.pallas_call(functools.partial(tile_kernel, group), grid_spec=pltpu.Pre...  22.5 us
    pallas_call x1, Pallas kernels, item_call(): pl.pallas_call(functools.partial(item_kernel, group), grid_spec=pltpu.Pre...  20 us
    pallas_call x2, Pallas kernels, owner_sum(): pl.pallas_call(functools.partial(owner_kernel, rank, scale), in_specs=[pl...  7.41 us
    pallas_call x1, Pallas kernels, user_grad_call(): pl.pallas_call(user_grad_kernel, in_specs=[any_space] * 3, out_specs=any_...  6.29 us
  transfers between devices with their start and end apart: 5, of which 4 were waited for; matrix products, arithmetic and copies ran while one was open for 3% of the time, Pallas kernels for 17%

profile of v4, /device:TPU:1, one launch (start us, length us, event | category | flops | bytes accessed | tf_op | source)
XLA Modules:
  0.0 302.4 jit_solution(11434062991234154751)
XLA Ops:
  0.6 0.8 pad_add_fusion
  1.6 20.8 %all_to_all.37 = s32[128,1,2]{2,1,0:T(1,128)S(1)} all-to-all(s32[128,1,2]{2,1,0:T(1,128)S(1)} %bitcast.29), channel_id=1, replica_groups=mesh['tm'=16,'rows'=8] {'tm','rows'}, dimensions={0} | all-to-all | bytes 2048 | tf_op jit(solution)/shard_map/all_to_all | solution.py:371
  22.4 0.7 slice_reduce_fusion
  23.1 3.0 %asked.3 = f32[128,64,128]{2,1,0:T(8,128)} custom-call(s32[128]{0:T(128)} %get-tuple-element.48.held, f32[8,64,128]{2,1,0:T(8,128)} %table.3), custom_call_target="tpu_custom_call" | custom-call | bytes 10000000 | tf_op jit(solution)/shard_map/asked/pallas_call | solution.py:283
  26.1 5.5 %all-to-all-start.1 = ((f32[128,64,128]{2,1,0:T(8,128)}), f32[128,64,128]{2,1,0:T(8,128)}, u32[]{:S(2)}, u32[]{:S(2)}) async-start(f32[128,64,128]{2,1,0:T(8,128)} %asked.3), calls=%async_computation.1 | async-start | bytes 8388608 | tf_op jit(solution)/shard_map/all_to_all | solution.py:371
  31.6 4.9 %fusion.3 = f32[8,64,64]{2,0,1:T(8,128)S(1)} fusion(f32[64,64,64]{2,1,0:T(8,128)S(1)} %copy-done, f32[8,64]{1,0:T(8,128)S(1)} %copy-done.3), kind=kOutput, calls=%fused_computation.12 | convolution fusion | flops 25165824 | bytes 1181696 | tf_op jit(solution)/shard_map/pqr,sr->spq/dot_general | solution.py:402
  36.6 3.0 %asked.2 = f32[128,64,128]{2,1,0:T(8,128)} custom-call(s32[128]{0:T(128)} %get-tuple-element.49.held, f32[8,64,128]{2,1,0:T(8,128)} %table.2), custom_call_target="tpu_custom_call" | custom-call | bytes 10000000 | tf_op jit(solution)/shard_map/asked/pallas_call | solution.py:283
  39.6 44.7 %all-to-all-done.1.items = f32[128,64,128]{2,1,0:T(8,128)} async-done(((f32[128,64,128]{2,1,0:T(8,128)}), f32[128,64,128]{2,1,0:T(8,128)}, u32[]{:S(2)}, u32[]{:S(2)}) %all-to-all-start.1) | async-done | bytes 4194336 | tf_op jit(solution)/shard_map/all_to_all | solution.py:371
  84.3 6.1 %all-to-all-start.2 = ((f32[128,64,128]{2,1,0:T(8,128)}), f32[128,64,128]{2,1,0:T(8,128)}, u32[]{:S(2)}, u32[]{:S(2)}) async-start(f32[128,64,128]{2,1,0:T(8,128)} %asked.2), calls=%async_computation.2 | async-start | bytes 8388608 | tf_op jit(solution)/shard_map/all_to_all | solution.py:371
  91.1 0.8 copy.55.cores
  91.8 20.0 %item_side.1 = (bf16[128,64,128]{2,1,0:T(8,128)(2,1)}, f32[128,64,128]{2,1,0:T(8,128)}, bf16[512,128,128]{2,1,0:T(8,128)(2,1)}, bf16[128,128,128]{2,1,0:T(8,128)(2,1)}) custom-call(s32[512]{0:T(512)} %slots_user.3, s32[512]{0:T(512)} %slots_item.3, s32[512]{0:T(512)} %steps.3, s32[1]{0:T(128)S(6)} %copy.68.count, f32[128,64,128]{2,1,0:T(8,128)} %all-to-all-done.1.items, ...), custom_call_target="tpu_custom_call" | custom-call | flops 20000000000 | bytes 50000000 | tf_op jit(solution)/shard_map/item_side/pallas_call | solution.py:121
  111.8 31.2 %all-to-all-done.2.users = f32[128,64,128]{2,1,0:T(8,128)} async-done(((f32[128,64,128]{2,1,0:T(8,128)}), f32[128,64,128]{2,1,0:T(8,128)}, u32[]{:S(2)}, u32[]{:S(2)}) %all-to-all-start.2) | async-done | bytes 4194336 | tf_op jit(solution)/shard_map/all_to_all | solution.py:371
  143.0 6.3 %user_grad.1 = f32[128,64,128]{2,1,0:T(8,128)} custom-call(f32[128,64,128]{2,1,0:T(8,128)} %all-to-all-done.2.users, bf16[128,64,128]{2,1,0:T(8,128)(2,1)} %get-tuple-element.35.gram, f32[128,64,128]{2,1,0:T(8,128)} %get-tuple-element.36.moved), custom_call_target="tpu_custom_call" | custom-call | flops 1000000000 | bytes 20000000 | tf_op jit(solution)/shard_map/user_grad/pallas_call | solution.py:176
  149.2 6.1 %all-to-all-start.3 = ((f32[128,64,128]{2,1,0:T(8,128)}), f32[128,64,128]{2,1,0:T(8,128)}, u32[]{:S(2)}, u32[]{:S(2)}) async-start(f32[128,64,128]{2,1,0:T(8,128)} %user_grad.1), calls=%async_computation.3 | async-start | bytes 8388608 | tf_op jit(solution)/shard_map/all_to_all | solution.py:371
  155.4 22.5 %tile_side.1 = (f32[128,72,128]{2,1,0:T(8,128)}, f32[8,64,64]{2,1,0:T(8,128)}) custom-call(s32[512]{0:T(512)} %slots_user.3, s32[512]{0:T(512)} %slots_item.3, s32[512]{0:T(512)} %steps.3, s32[1]{0:T(128)S(6)} %copy.68.count, f32[128,64,128]{2,1,0:T(8,128)} %all-to-all-done.2.users, bf16[128,128,128]{2,1,0:T(8,128)(2,1)} %get-tuple-element.38.right, ...), custom_call_target="tpu_custom_call" | custom-call | flops 30000001024 | bytes 50000000 | tf_op jit(solution)/shard_map/tile_side/pallas_call | solution.py:244
  177.9 1.1 reshape.74
  179.0 2.2 convolution_bitcast_fusion
  181.2 0.2 copy.57
  181.8 26.1 %all-to-all-done.3.back = f32[128,64,128]{2,1,0:T(8,128)} async-done(((f32[128,64,128]{2,1,0:T(8,128)}), f32[128,64,128]{2,1,0:T(8,128)}, u32[]{:S(2)}, u32[]{:S(2)}) %all-to-all-start.3) | async-done | bytes 4194336 | tf_op jit(solution)/shard_map/all_to_all | solution.py:371
  207.9 18.9 %all_to_all.38 = f32[128,8,128]{2,1,0:T(8,128)S(1)} all-to-all(f32[128,8,128]{2,1,0:T(8,128)S(1)} %pad_maximum_fusion), channel_id=1, replica_groups=mesh['tm'=16,'rows'=8] {'tm','rows'}, dimensions={0} | all-to-all | bytes 1048576 | tf_op jit(solution)/shard_map/all_to_all | solution.py:371
  226.8 0.2 reshape.77
  227.1 0.3 convolution_multiply_fusion
  227.6 0.9 constant_dynamic-update-slice_fusion
  228.4 5.6 %all-to-all-start.5 = ((f32[128,72,128]{2,1,0:T(8,128)}), f32[128,72,128]{2,1,0:T(8,128)}, u32[]{:S(2)}, u32[]{:S(2)}) async-start(f32[128,72,128]{2,1,0:T(8,128)} %constant_dynamic-update-slice_fusion), calls=%async_computation.5 | async-start | bytes 9437184 | tf_op jit(solution)/shard_map/all_to_all | solution.py:371
  234.0 3.7 %owner_sum.2 = f32[8,64,128]{2,1,0:T(8,128)} custom-call(s32[128]{0:T(128)} %get-tuple-element.49.held, f32[128,64,128]{2,1,0:T(8,128)} %all-to-all-done.3.back), custom_call_target="tpu_custom_call" | custom-call | flops 10000000 | bytes 10000000 | tf_op jit(solution)/shard_map/owner_sum/pallas_call | solution.py:325
  237.8 0.7 mul.23
  238.5 54.3 %all-to-all-done.5.back = f32[128,72,128]{2,1,0:T(8,128)} async-done(((f32[128,72,128]{2,1,0:T(8,128)}), f32[128,72,128]{2,1,0:T(8,128)}, u32[]{:S(2)}, u32[]{:S(2)}) %all-to-all-start.5) | async-done | bytes 4718624 | tf_op jit(solution)/shard_map/all_to_all | solution.py:371
  292.7 1.1 slice.45.mine
  293.8 1.2 collective-permute-start
  295.0 3.7 %owner_sum.3 = f32[8,64,128]{2,1,0:T(8,128)} custom-call(s32[128]{0:T(128)} %get-tuple-element.48.held, f32[128,72,128]{2,1,0:T(8,128)} %all-to-all-done.5.back), custom_call_target="tpu_custom_call" | custom-call | flops 10000000 | bytes 10000000 | tf_op jit(solution)/shard_map/owner_sum/pallas_call | solution.py:325
  298.8 0.8 copy-done.2
  299.5 2.9 core_unpack.1
  (24 shorter events, 0.9 us)
Async XLA Ops:
  0.6 31.0 %copy-start = (f32[64,64,64]{2,1,0:T(8,128)S(1)}, f32[64,64,64]{2,1,0:T(8,128)}, u32[]{:S(2)}) copy-start(f32[64,64,64]{2,1,0:T(8,128)} %param.23) | copy-start | bytes 3145732
  26.1 5.5 %copy-start.3 = (f32[8,64]{1,0:T(8,128)S(1)}, f32[8,64]{1,0:T(8,128)}, u32[]{:S(2)}) copy-start(f32[8,64]{1,0:T(8,128)} %param.22) | copy-start | bytes 6148
  26.1 58.1 %all-to-all-start.1 = ((f32[128,64,128]{2,1,0:T(8,128)}), f32[128,64,128]{2,1,0:T(8,128)}, u32[]{:S(2)}, u32[]{:S(2)}) async-start(f32[128,64,128]{2,1,0:T(8,128)} %asked.3), calls=%async_computation.1 | async-start | bytes 8388608 | tf_op jit(solution)/shard_map/all_to_all | solution.py:371
  84.3 58.7 %all-to-all-start.2 = ((f32[128,64,128]{2,1,0:T(8,128)}), f32[128,64,128]{2,1,0:T(8,128)}, u32[]{:S(2)}, u32[]{:S(2)}) async-start(f32[128,64,128]{2,1,0:T(8,128)} %asked.2), calls=%async_computation.2 | async-start | bytes 8388608 | tf_op jit(solution)/shard_map/all_to_all | solution.py:371
  149.2 58.6 %all-to-all-start.3 = ((f32[128,64,128]{2,1,0:T(8,128)}), f32[128,64,128]{2,1,0:T(8,128)}, u32[]{:S(2)}, u32[]{:S(2)}) async-start(f32[128,64,128]{2,1,0:T(8,128)} %user_grad.1), calls=%async_computation.3 | async-start | bytes 8388608 | tf_op jit(solution)/shard_map/all_to_all | solution.py:371
  228.4 64.3 %all-to-all-start.5 = ((f32[128,72,128]{2,1,0:T(8,128)}), f32[128,72,128]{2,1,0:T(8,128)}, u32[]{:S(2)}, u32[]{:S(2)}) async-start(f32[128,72,128]{2,1,0:T(8,128)} %constant_dynamic-update-slice_fusion), calls=%async_computation.5 | async-start | bytes 9437184 | tf_op jit(solution)/shard_map/all_to_all | solution.py:371
  293.8 4.9 %copy-start.1 = (f32[128,8,128]{2,1,0:T(8,128)}, f32[128,8,128]{2,1,0:T(8,128)S(1)}, u32[]{:S(2)}) copy-start(f32[128,8,128]{2,1,0:T(8,128)S(1)} %slice.45.mine) | copy-start | bytes 1572868
  293.8 4.9 %collective-permute-start = (f32[128,8,128]{2,1,0:T(8,128)S(1)}, f32[128,8,128]{2,1,0:T(8,128)S(1)}, u32[]{:S(2)}, u32[]{:S(2)}) collective-permute-start(f32[128,8,128]{2,1,0:T(8,128)S(1)} %slice.45.mine), channel_id=1, source_target_pairs={{0,1},{1,0},{2,3},{3,2},{4,5},{5,4},{6,7},{7,6},{8,9},{9,8},{10,11... | collective-permute-start | bytes 1572872 | tf_op jit(solution)/shard_map/ppermute | solution.py:437
  298.7 0.8 copy-start.2

commit v5 on v4

--- a/solution.py
+++ b/solution.py
@@ -369,6 +369,11 @@
 
 def to_all(x):
     return lax.all_to_all(x, AXES, split_axis=0, concat_axis=0, tiled=True)
+
+
+def from_row(x, distance):
+    count = lax.axis_size("rows")
+    return lax.ppermute(x, "rows", [(r, r ^ distance) for r in range(count)])
 
 
 def shards(
@@ -393,7 +398,6 @@
     owners = count_tm * count_rows
     part = rank * rank // owners
     sum_rows = step_count * part // width
-    time_rows = step_count * rank // width
     core_rows = part * rank // width // 2
     asks = to_all(cat([users_ask, items_ask], 1))
     held_user, held_item = asks[:, 0], asks[:, 1]
@@ -414,9 +418,8 @@
     parts = step_sums.reshape(step_count, owners, part).transpose(1, 0, 2).reshape(owners, sum_rows, width)
     row = lax.dynamic_slice_in_dim(time_factor, lax.axis_index("rows"), 1, 0)
     row = jnp.pad(row, ((0, 0), (0, width - rank)))
-    own_time = jnp.einsum("spq,pqr->sr", step_sums, core, precision=HIGH).reshape(time_rows, width)
-    blank = jnp.zeros((-(sum_rows + 1 + time_rows) % 8, width), F32)
-    shared = cat([row, own_time, blank], 0)
+    blank = jnp.zeros((-(sum_rows + 1) % 4, width), F32)
+    shared = cat([row, blank], 0)
     sent = cat([parts, jnp.broadcast_to(shared[None], (owners,) + shared.shape)], 1)
     sent, back_left = lax.optimization_barrier((sent, back_left))
     got = to_all(sent)
@@ -428,13 +431,15 @@
     own = jnp.broadcast_to(own, (owners // 2, 2, core_rows, width)).reshape(owners, core_rows, width)
     slot_right = slot_right.at[:, rank:].set(own)
     back_right = to_all(slot_right)
-    first = lax.axis_index("tm") * count_rows
-    terms = lax.dynamic_slice_in_dim(got, first, count_rows, 0)[:, sum_rows + 1 : sum_rows + 1 + time_rows]
-    grad_time = time_scale * jnp.sum(terms, axis=0).reshape(step_count, rank)
     grad_users = owner_sum(held_user, back_left, blocks_own, rank, user_scale)
+    step_sums, grad_users = lax.optimization_barrier((step_sums, grad_users))
+    own_time = jnp.einsum("spq,pqr->sr", step_sums, core, precision=HIGH)
+    for distance in [1 << k for k in range(count_rows.bit_length() - 1)]:
+        own_time = own_time + from_row(own_time, distance)
+    grad_time = time_scale * own_time
     back_right, grad_users, grad_time = lax.optimization_barrier((back_right, grad_users, grad_time))
     mine = back_right[:, rank:]
-    other = lax.ppermute(mine, "rows", [(r, r ^ 1) for r in range(count_rows)])
+    other = from_row(mine, 1)
     grad_items = owner_sum(held_item, back_right, blocks_own, rank, user_scale)
     odd = (lax.axis_index("rows") % 2).astype(jnp.int32).reshape(1)
     grad_core = core_unpack(odd, mine, other).reshape(rank, rank, rank)

time: 303 us -> 302 us (level)
  starting transfers between devices: 24.4 us -> 29 us
    all_to_all x4, waiting for transfers between devices: 156 us -> 105 us  [to_all(): return lax.all_to_all(x, AXES, split_axis=0, concat_axis=0, tiled=True)]
    ppermute x1 -> x4, waiting for transfers between devices: 0.01 us -> 47.4 us  [from_row(): return lax.ppermute(x, 'rows', [(r, r ^ distance) for r in range(count)])]
    ppermute x1 -> x4, starting transfers between devices: 1.19 us -> 5.92 us  [from_row(): return lax.ppermute(x, 'rows', [(r, r ^ distance) for r in range(count)])]
  transfers between devices with their start and end apart: 5 -> 8, of which waited for: 4 -> 7; matrix products, arithmetic and copies ran while one was open for 3% -> 3% of each run, Pallas kernels for 17% -> 18%
where the time goes in v5:
time: 302 us; the launch traced here: 300 us
  waiting for transfers between devices  153 us (51%)
  Pallas kernels  65.2 us (22%)
  blocking collectives  37.1 us (12%)
  starting transfers between devices  29 us (10%)
  matrix products  6.44 us (2%)
  local copies, waits for them, and re-layouts  6.35 us (2%)
    all_to_all x4, waiting for transfers between devices, to_all(): return lax.all_to_all(x, AXES, split_axis=0, concat_axis=0, tiled=True)  105 us
    ppermute x4, waiting for transfers between devices, from_row(): return lax.ppermute(x, 'rows', [(r, r ^ distance) for r in range(count)])  47.4 us
    all_to_all x2, blocking collectives, to_all(): return lax.all_to_all(x, AXES, split_axis=0, concat_axis=0, tiled=True)  37.1 us
    all_to_all x4, starting transfers between devices, to_all(): return lax.all_to_all(x, AXES, split_axis=0, concat_axis=0, tiled=True)  23.1 us
    pallas_call x1, Pallas kernels, tile_call(): pl.pallas_call(functools.partial(tile_kernel, group), grid_spec=pltpu.Pre...  22.5 us
    pallas_call x1, Pallas kernels, item_call(): pl.pallas_call(functools.partial(item_kernel, group), grid_spec=pltpu.Pre...  20 us
    pallas_call x2, Pallas kernels, owner_sum(): pl.pallas_call(functools.partial(owner_kernel, rank, scale), in_specs=[pl...  7.54 us
    pallas_call x1, Pallas kernels, user_grad_call(): pl.pallas_call(user_grad_kernel, in_specs=[any_space] * 3, out_specs=any_...  6.29 us
  transfers between devices with their start and end apart: 8, of which 7 were waited for; matrix products, arithmetic and copies ran while one was open for 3% of the time, Pallas kernels for 18%

profile of v5, /device:TPU:1, one launch (start us, length us, event | category | flops | bytes accessed | tf_op | source)
XLA Modules:
  0.0 299.8 jit_solution(9819306426848443046)
XLA Ops:
  0.6 0.8 pad_add_fusion
  1.6 20.8 %all_to_all.37 = s32[128,1,2]{2,1,0:T(1,128)S(1)} all-to-all(s32[128,1,2]{2,1,0:T(1,128)S(1)} %bitcast.29), channel_id=1, replica_groups=mesh['tm'=16,'rows'=8] {'tm','rows'}, dimensions={0} | all-to-all | bytes 2048 | tf_op jit(solution)/shard_map/all_to_all | solution.py:371
  23.1 3.0 %asked.3 = f32[128,64,128]{2,1,0:T(8,128)} custom-call(s32[128]{0:T(128)} %get-tuple-element.52.held, f32[8,64,128]{2,1,0:T(8,128)} %table.3), custom_call_target="tpu_custom_call" | custom-call | bytes 10000000 | tf_op jit(solution)/shard_map/asked/pallas_call | solution.py:283
  26.2 5.4 %all-to-all-start.1 = ((f32[128,64,128]{2,1,0:T(8,128)}), f32[128,64,128]{2,1,0:T(8,128)}, u32[]{:S(2)}, u32[]{:S(2)}) async-start(f32[128,64,128]{2,1,0:T(8,128)} %asked.3), calls=%async_computation.1 | async-start | bytes 8388608 | tf_op jit(solution)/shard_map/all_to_all | solution.py:371
  31.6 4.9 %fusion.2 = f32[8,64,64]{2,0,1:T(8,128)S(1)} fusion(f32[64,64,64]{2,1,0:T(8,128)S(1)} %copy-done, f32[8,64]{1,0:T(8,128)S(1)} %copy-done.4), kind=kOutput, calls=%fused_computation.8 | convolution fusion | flops 25165824 | bytes 1181696 | tf_op jit(solution)/shard_map/pqr,sr->spq/dot_general | solution.py:406
  36.6 3.0 %asked.2 = f32[128,64,128]{2,1,0:T(8,128)} custom-call(s32[128]{0:T(128)} %get-tuple-element.53.held, f32[8,64,128]{2,1,0:T(8,128)} %table.2), custom_call_target="tpu_custom_call" | custom-call | bytes 10000000 | tf_op jit(solution)/shard_map/asked/pallas_call | solution.py:283
  39.6 44.7 %all-to-all-done.1.items = f32[128,64,128]{2,1,0:T(8,128)} async-done(((f32[128,64,128]{2,1,0:T(8,128)}), f32[128,64,128]{2,1,0:T(8,128)}, u32[]{:S(2)}, u32[]{:S(2)}) %all-to-all-start.1) | async-done | bytes 4194336 | tf_op jit(solution)/shard_map/all_to_all | solution.py:371
  84.3 6.1 %all-to-all-start.2 = ((f32[128,64,128]{2,1,0:T(8,128)}), f32[128,64,128]{2,1,0:T(8,128)}, u32[]{:S(2)}, u32[]{:S(2)}) async-start(f32[128,64,128]{2,1,0:T(8,128)} %asked.2), calls=%async_computation.2 | async-start | bytes 8388608 | tf_op jit(solution)/shard_map/all_to_all | solution.py:371
  91.1 0.8 copy.46.cores
  91.8 20.0 %item_side.1 = (bf16[128,64,128]{2,1,0:T(8,128)(2,1)}, f32[128,64,128]{2,1,0:T(8,128)}, bf16[512,128,128]{2,1,0:T(8,128)(2,1)}, bf16[128,128,128]{2,1,0:T(8,128)(2,1)}) custom-call(s32[512]{0:T(512)} %slots_user.3, s32[512]{0:T(512)} %slots_item.3, s32[512]{0:T(512)} %steps.3, s32[1]{0:T(128)S(6)} %copy.57.count, f32[128,64,128]{2,1,0:T(8,128)} %all-to-all-done.1.items, ...), custom_call_target="tpu_custom_call" | custom-call | flops 20000000000 | bytes 50000000 | tf_op jit(solution)/shard_map/item_side/pallas_call | solution.py:121
  111.8 31.1 %all-to-all-done.2.users = f32[128,64,128]{2,1,0:T(8,128)} async-done(((f32[128,64,128]{2,1,0:T(8,128)}), f32[128,64,128]{2,1,0:T(8,128)}, u32[]{:S(2)}, u32[]{:S(2)}) %all-to-all-start.2) | async-done | bytes 4194336 | tf_op jit(solution)/shard_map/all_to_all | solution.py:371
  143.0 6.3 %user_grad.1 = f32[128,64,128]{2,1,0:T(8,128)} custom-call(f32[128,64,128]{2,1,0:T(8,128)} %all-to-all-done.2.users, bf16[128,64,128]{2,1,0:T(8,128)(2,1)} %get-tuple-element.37.gram, f32[128,64,128]{2,1,0:T(8,128)} %get-tuple-element.38.moved), custom_call_target="tpu_custom_call" | custom-call | flops 1000000000 | bytes 20000000 | tf_op jit(solution)/shard_map/user_grad/pallas_call | solution.py:176
  149.3 6.1 %all-to-all-start.3 = ((f32[128,64,128]{2,1,0:T(8,128)}), f32[128,64,128]{2,1,0:T(8,128)}, u32[]{:S(2)}, u32[]{:S(2)}) async-start(f32[128,64,128]{2,1,0:T(8,128)} %user_grad.1), calls=%async_computation.3 | async-start | bytes 8388608 | tf_op jit(solution)/shard_map/all_to_all | solution.py:371
  155.4 22.5 %tile_side.1 = (f32[128,72,128]{2,1,0:T(8,128)}, f32[8,64,64]{2,1,0:T(8,128)}) custom-call(s32[512]{0:T(512)} %slots_user.3, s32[512]{0:T(512)} %slots_item.3, s32[512]{0:T(512)} %steps.3, s32[1]{0:T(128)S(6)} %copy.57.count, f32[128,64,128]{2,1,0:T(8,128)} %all-to-all-done.2.users, bf16[128,128,128]{2,1,0:T(8,128)(2,1)} %get-tuple-element.40.right, ...), custom_call_target="tpu_custom_call" | custom-call | flops 30000001024 | bytes 50000000 | tf_op jit(solution)/shard_map/tile_side/pallas_call | solution.py:244
  177.8 1.1 reshape.68
  179.2 28.6 %all-to-all-done.3.back = f32[128,64,128]{2,1,0:T(8,128)} async-done(((f32[128,64,128]{2,1,0:T(8,128)}), f32[128,64,128]{2,1,0:T(8,128)}, u32[]{:S(2)}, u32[]{:S(2)}) %all-to-all-start.3) | async-done | bytes 4194336 | tf_op jit(solution)/shard_map/all_to_all | solution.py:371
  208.0 16.3 %all_to_all.38 = f32[128,4,128]{2,1,0:T(4,128)S(1)} all-to-all(f32[128,4,128]{2,1,0:T(4,128)S(1)} %copy.49), channel_id=1, replica_groups=mesh['tm'=16,'rows'=8] {'tm','rows'}, dimensions={0} | all-to-all | bytes 524288 | tf_op jit(solution)/shard_map/all_to_all | solution.py:371
  225.1 0.9 constant_dynamic-update-slice_fusion
  226.0 5.4 %all-to-all-start.5 = ((f32[128,72,128]{2,1,0:T(8,128)}), f32[128,72,128]{2,1,0:T(8,128)}, u32[]{:S(2)}, u32[]{:S(2)}) async-start(f32[128,72,128]{2,1,0:T(8,128)} %constant_dynamic-update-slice_fusion), calls=%async_computation.5 | async-start | bytes 9437184 | tf_op jit(solution)/shard_map/all_to_all | solution.py:371
  231.5 3.8 %owner_sum.2 = f32[8,64,128]{2,1,0:T(8,128)} custom-call(s32[128]{0:T(128)} %get-tuple-element.53.held, f32[128,64,128]{2,1,0:T(8,128)} %all-to-all-done.3.back), custom_call_target="tpu_custom_call" | custom-call | flops 10000000 | bytes 10000000 | tf_op jit(solution)/shard_map/owner_sum/pallas_call | solution.py:325
  235.3 1.2 convolution_bitcast_fusion
  236.6 1.4 collective-permute-start
  237.9 0.8 collective-permute-done
  239.3 45.1 %collective-permute-done.1 = f32[8,64]{1,0:T(8,128)S(1)} collective-permute-done((f32[8,64]{1,0:T(8,128)S(1)}, f32[8,64]{1,0:T(8,128)S(1)}, u32[]{:S(2)}, u32[]{:S(2)}) %collective-permute-start.1) | collective-permute-done | bytes 2080 | tf_op jit(solution)/shard_map/ppermute | solution.py:376
  284.3 2.9 collective-permute-start.2
  287.2 1.5 collective-permute-done.2
  289.3 0.9 all-to-all-done.5.back
  290.2 1.1 slice.41.mine
  291.2 1.2 collective-permute-start.3
  292.4 3.7 %owner_sum.3 = f32[8,64,128]{2,1,0:T(8,128)} custom-call(s32[128]{0:T(128)} %get-tuple-element.52.held, f32[128,72,128]{2,1,0:T(8,128)} %all-to-all-done.5.back), custom_call_target="tpu_custom_call" | custom-call | flops 10000000 | bytes 10000000 | tf_op jit(solution)/shard_map/owner_sum/pallas_call | solution.py:325
  296.2 0.8 copy-done.3
  296.9 2.9 core_unpack.1
  (30 shorter events, 3.2 us)
Async XLA Ops:
  0.6 31.0 %copy-start = (f32[64,64,64]{2,1,0:T(8,128)S(1)}, f32[64,64,64]{2,1,0:T(8,128)}, u32[]{:S(2)}) copy-start(f32[64,64,64]{2,1,0:T(8,128)} %param.23) | copy-start | bytes 3145732
  26.1 5.5 %copy-start.4 = (f32[8,64]{1,0:T(8,128)S(1)}, f32[8,64]{1,0:T(8,128)}, u32[]{:S(2)}) copy-start(f32[8,64]{1,0:T(8,128)} %param.22) | copy-start | bytes 6148
  26.2 58.1 %all-to-all-start.1 = ((f32[128,64,128]{2,1,0:T(8,128)}), f32[128,64,128]{2,1,0:T(8,128)}, u32[]{:S(2)}, u32[]{:S(2)}) async-start(f32[128,64,128]{2,1,0:T(8,128)} %asked.3), calls=%async_computation.1 | async-start | bytes 8388608 | tf_op jit(solution)/shard_map/all_to_all | solution.py:371
  84.3 58.7 %all-to-all-start.2 = ((f32[128,64,128]{2,1,0:T(8,128)}), f32[128,64,128]{2,1,0:T(8,128)}, u32[]{:S(2)}, u32[]{:S(2)}) async-start(f32[128,64,128]{2,1,0:T(8,128)} %asked.2), calls=%async_computation.2 | async-start | bytes 8388608 | tf_op jit(solution)/shard_map/all_to_all | solution.py:371
  149.3 58.6 %all-to-all-start.3 = ((f32[128,64,128]{2,1,0:T(8,128)}), f32[128,64,128]{2,1,0:T(8,128)}, u32[]{:S(2)}, u32[]{:S(2)}) async-start(f32[128,64,128]{2,1,0:T(8,128)} %user_grad.1), calls=%async_computation.3 | async-start | bytes 8388608 | tf_op jit(solution)/shard_map/all_to_all | solution.py:371
  226.0 64.1 %all-to-all-start.5 = ((f32[128,72,128]{2,1,0:T(8,128)}), f32[128,72,128]{2,1,0:T(8,128)}, u32[]{:S(2)}, u32[]{:S(2)}) async-start(f32[128,72,128]{2,1,0:T(8,128)} %constant_dynamic-update-slice_fusion), calls=%async_computation.5 | async-start | bytes 9437184 | tf_op jit(solution)/shard_map/all_to_all | solution.py:371
  231.5 3.9 %copy-start.2 = (f32[8,64,64]{2,1,0:T(8,128)S(1)}, f32[8,64,64]{2,1,0:T(8,128)}, u32[]{:S(2)}) copy-start(f32[8,64,64]{2,1,0:T(8,128)} %get-tuple-element.48) | copy-start | bytes 393220
  236.6 2.2 collective-permute-start
  238.7 45.6 %collective-permute-start.1 = (f32[8,64]{1,0:T(8,128)S(1)}, f32[8,64]{1,0:T(8,128)S(1)}, u32[]{:S(2)}, u32[]{:S(2)}) collective-permute-start(f32[8,64]{1,0:T(8,128)S(1)} %add.23), channel_id=1, source_target_pairs={{0,2},{1,3},{2,0},{3,1},{4,6},{5,7},{6,4},{7,5},{8,10},{9,11},{10,... | collective-permute-start | bytes 6152 | tf_op jit(solution)/shard_map/ppermute | solution.py:376
  284.3 4.4 %collective-permute-start.2 = (f32[8,64]{1,0:T(8,128)S(1)}, f32[8,64]{1,0:T(8,128)S(1)}, u32[]{:S(2)}, u32[]{:S(2)}) collective-permute-start(f32[8,64]{1,0:T(8,128)S(1)} %add.24), channel_id=1, source_target_pairs={{0,4},{1,5},{2,6},{3,7},{4,0},{5,1},{6,2},{7,3},{8,12},{9,13},{10,... | collective-permute-start | bytes 6152 | tf_op jit(solution)/shard_map/ppermute | solution.py:376
  291.2 4.9 %copy-start.1 = (f32[128,8,128]{2,1,0:T(8,128)}, f32[128,8,128]{2,1,0:T(8,128)S(1)}, u32[]{:S(2)}) copy-start(f32[128,8,128]{2,1,0:T(8,128)S(1)} %slice.41.mine) | copy-start | bytes 1572868
  291.2 4.9 %collective-permute-start.3 = (f32[128,8,128]{2,1,0:T(8,128)S(1)}, f32[128,8,128]{2,1,0:T(8,128)S(1)}, u32[]{:S(2)}, u32[]{:S(2)}) collective-permute-start(f32[128,8,128]{2,1,0:T(8,128)S(1)} %slice.41.mine), channel_id=1, source_target_pairs={{0,1},{1,0},{2,3},{3,2},{4,5},{5,4},{6,7},{7,6},{8,9},{9,8},{10,11... | collective-permute-start | bytes 1572872 | tf_op jit(solution)/shard_map/ppermute | solution.py:376
  296.2 0.8 copy-start.3

commit v6 on v5

--- a/solution.py
+++ b/solution.py
@@ -335,36 +335,67 @@
     )(held, back)
 
 
-def core_kernel(odd, mine, other, core):
-    half = mine.shape[2] // 2
-    rows = 2 * mine.shape[1]
-
-    def step(ks):
-        a = [mine[k] for k in ks]
-        b = [other[k] for k in ks]
-        new = []
-        for x, y in zip(a, b):
-            new.append((jnp.where(odd[0] == 0, x, y), jnp.where(odd[0] == 0, y, x)))
-        new = [[cat([x[:, :half], x[:, half:]], 0) for x in pair] for pair in new]
-        for k, (x, y) in zip(ks, new):
-            core[k, :rows] = x
-            core[k, rows:] = y
-
+def owner_core_kernel(rank, scale, held, odd, back, mine, other, out, core, *rest):
+    adders, (back_v, core_v, sems, core_sem) = rest[:ADDERS], rest[ADDERS:]
+    size = back_v.shape[0] // CHUNKS
+    half, rows = mine.shape[2] // 2, 2 * mine.shape[1]
+
+    def fetch(c):
+        at = pl.ds(c * size, size)
+        return pltpu.make_async_copy(back.at[at, pl.ds(0, rank)], back_v.at[at], sems.at[c])
+
+    for c in range(CHUNKS):
+        fetch(c).start()
+    for a in adders:
+        a[...] = jnp.zeros_like(a)
     for g in range(0, mine.shape[0], PREP):
-        step(range(g, g + PREP))
-
-
-def core_unpack(odd, mine, other):
-    owners, rows, width = mine.shape
-    return pl.pallas_call(
-        core_kernel,
-        in_specs=[pl.BlockSpec(memory_space=pltpu.SMEM)] + [pl.BlockSpec(memory_space=pltpu.VMEM)] * 2,
-        out_specs=pl.BlockSpec(memory_space=pltpu.VMEM),
-        out_shape=jax.ShapeDtypeStruct((owners, 4 * rows, width // 2), F32),
-        compiler_params=pltpu.CompilerParams(vmem_limit_bytes=60 * 2**20),
-        cost_estimate=pl.CostEstimate(flops=10**6, bytes_accessed=3 * 10**6, transcendentals=0),
-        name="core_unpack",
-    )(odd, mine, other)
+        span = range(g, g + PREP)
+        pair = [(mine[k], other[k]) for k in span]
+        pair = [(jnp.where(odd[0] == 0, x, y), jnp.where(odd[0] == 0, y, x)) for x, y in pair]
+        pair = [[cat([x[:, :half], x[:, half:]], 0) for x in both] for both in pair]
+        for k, (x, y) in zip(span, pair):
+            core_v[k, :rows] = x
+            core_v[k, rows:] = y
+    leave = pltpu.make_async_copy(core_v, core, core_sem)
+    leave.start()
+    for c in range(CHUNKS):
+        fetch(c).wait()
+        for t in range(c * size, (c + 1) * size, ADDERS):
+            at = [held[t + k] for k in range(ADDERS)]
+            new = [adders[k][at[k]] + back_v[t + k] for k in range(ADDERS)]
+            for k in range(ADDERS):
+                adders[k][at[k]] = new[k]
+    total = adders[0][...]
+    for a in adders[1:]:
+        total = total + a[...]
+    out[...] = scale * total
+    leave.wait()
+
+
+def owner_core_sum(held, odd, back, mine, other, blocks_own, rank, scale):
+    total, rows, width = back.shape
+    core_shape = (total, 4 * mine.shape[1], width // 2)
+    small, local = pl.BlockSpec(memory_space=pltpu.SMEM), pl.BlockSpec(memory_space=pltpu.VMEM)
+    far = pl.BlockSpec(memory_space=pltpu.HBM)
+    return pl.pallas_call(
+        functools.partial(owner_core_kernel, rank, scale),
+        in_specs=[small, small, far, local, local],
+        out_specs=[local, far],
+        out_shape=[
+            jax.ShapeDtypeStruct((blocks_own, rank, width), F32),
+            jax.ShapeDtypeStruct(core_shape, F32),
+        ],
+        scratch_shapes=[pltpu.VMEM((blocks_own, rank, width), F32) for _ in range(ADDERS)]
+        + [
+            pltpu.VMEM((total, rank, width), F32),
+            pltpu.VMEM(core_shape, F32),
+            pltpu.SemaphoreType.DMA((CHUNKS,)),
+            pltpu.SemaphoreType.DMA,
+        ],
+        compiler_params=pltpu.CompilerParams(vmem_limit_bytes=40 * 2**20),
+        cost_estimate=pl.CostEstimate(flops=10**7, bytes_accessed=10**7, transcendentals=0),
+        name="owner_core_sum",
+    )(held, odd, back, mine, other)
 
 
 def to_all(x):
@@ -440,9 +471,11 @@
     back_right, grad_users, grad_time = lax.optimization_barrier((back_right, grad_users, grad_time))
     mine = back_right[:, rank:]
     other = from_row(mine, 1)
-    grad_items = owner_sum(held_item, back_right, blocks_own, rank, user_scale)
     odd = (lax.axis_index("rows") % 2).astype(jnp.int32).reshape(1)
-    grad_core = core_unpack(odd, mine, other).reshape(rank, rank, rank)
+    grad_items, grad_core = owner_core_sum(
+        held_item, odd, back_right, mine, other, blocks_own, rank, user_scale
+    )
+    grad_core = grad_core.reshape(rank, rank, rank)
     return (grad_users, grad_items, grad_time, grad_core)
 
 

time: 302 us -> 301 us (level)
    pallas_call x2 -> x1, Pallas kernels: 7.54 us -> 3.84 us  [owner_sum(): pl.pallas_call(functools.partial(owner_kernel, rank, scale), in_specs=[pl...]
  transfers between devices with their start and end apart: 8 -> 8, of which waited for: 7 -> 8; matrix products, arithmetic and copies ran while one was open for 3% -> 3% of each run, Pallas kernels for 18% -> 17%
where the time goes in v6:
time: 301 us; the launch traced here: 299 us
  waiting for transfers between devices  154 us (51%)
  Pallas kernels  63.2 us (21%)
  blocking collectives  37.1 us (12%)
  starting transfers between devices  29 us (10%)
  matrix products  6.44 us (2%)
  local copies, waits for them, and re-layouts  5.58 us (2%)
    all_to_all x4, waiting for transfers between devices, to_all(): return lax.all_to_all(x, AXES, split_axis=0, concat_axis=0, tiled=True)  105 us
    ppermute x4, waiting for transfers between devices, from_row(): return lax.ppermute(x, 'rows', [(r, r ^ distance) for r in range(count)])  48.9 us
    all_to_all x2, blocking collectives, to_all(): return lax.all_to_all(x, AXES, split_axis=0, concat_axis=0, tiled=True)  37.1 us
    all_to_all x4, starting transfers between devices, to_all(): return lax.all_to_all(x, AXES, split_axis=0, concat_axis=0, tiled=True)  23.1 us
    pallas_call x1, Pallas kernels, tile_call(): pl.pallas_call(functools.partial(tile_kernel, group), grid_spec=pltpu.Pre...  22.5 us
    pallas_call x1, Pallas kernels, item_call(): pl.pallas_call(functools.partial(item_kernel, group), grid_spec=pltpu.Pre...  20 us
    pallas_call x1, Pallas kernels, user_grad_call(): pl.pallas_call(user_grad_kernel, in_specs=[any_space] * 3, out_specs=any_...  6.29 us
    pallas_call x2, Pallas kernels, asked(): pl.pallas_call(ask_kernel, in_specs=[pl.BlockSpec(memory_space=pltpu.SMEM...  6.07 us
  transfers between devices with their start and end apart: 8, of which 8 were waited for; matrix products, arithmetic and copies ran while one was open for 3% of the time, Pallas kernels for 17%

profile of v6, /device:TPU:1, one launch (start us, length us, event | category | flops | bytes accessed | tf_op | source)
XLA Modules:
  0.0 298.7 jit_solution(10116049294569507410)
XLA Ops:
  0.6 0.8 pad_add_fusion
  1.6 20.8 %all_to_all.37 = s32[128,1,2]{2,1,0:T(1,128)S(1)} all-to-all(s32[128,1,2]{2,1,0:T(1,128)S(1)} %bitcast.28), channel_id=1, replica_groups=mesh['tm'=16,'rows'=8] {'tm','rows'}, dimensions={0} | all-to-all | bytes 2048 | tf_op jit(solution)/shard_map/all_to_all | solution.py:402
  22.4 0.7 slice_reduce_fusion
  23.1 3.0 %asked.3 = f32[128,64,128]{2,1,0:T(8,128)} custom-call(s32[128]{0:T(128)} %get-tuple-element.56.held, f32[8,64,128]{2,1,0:T(8,128)} %table.3), custom_call_target="tpu_custom_call" | custom-call | bytes 10000000 | tf_op jit(solution)/shard_map/asked/pallas_call | solution.py:283
  26.2 5.4 %all-to-all-start.1 = ((f32[128,64,128]{2,1,0:T(8,128)}), f32[128,64,128]{2,1,0:T(8,128)}, u32[]{:S(2)}, u32[]{:S(2)}) async-start(f32[128,64,128]{2,1,0:T(8,128)} %asked.3), calls=%async_computation.1 | async-start | bytes 8388608 | tf_op jit(solution)/shard_map/all_to_all | solution.py:402
  31.6 4.9 %fusion.2 = f32[8,64,64]{2,0,1:T(8,128)S(1)} fusion(f32[64,64,64]{2,1,0:T(8,128)S(1)} %copy-done, f32[8,64]{1,0:T(8,128)S(1)} %copy-done.3), kind=kOutput, calls=%fused_computation.8 | convolution fusion | flops 25165824 | bytes 1181696 | tf_op jit(solution)/shard_map/pqr,sr->spq/dot_general | solution.py:437
  36.6 3.0 %asked.2 = f32[128,64,128]{2,1,0:T(8,128)} custom-call(s32[128]{0:T(128)} %get-tuple-element.57.held, f32[8,64,128]{2,1,0:T(8,128)} %table.2), custom_call_target="tpu_custom_call" | custom-call | bytes 10000000 | tf_op jit(solution)/shard_map/asked/pallas_call | solution.py:283
  39.6 44.7 %all-to-all-done.1.items = f32[128,64,128]{2,1,0:T(8,128)} async-done(((f32[128,64,128]{2,1,0:T(8,128)}), f32[128,64,128]{2,1,0:T(8,128)}, u32[]{:S(2)}, u32[]{:S(2)}) %all-to-all-start.1) | async-done | bytes 4194336 | tf_op jit(solution)/shard_map/all_to_all | solution.py:402
  84.3 6.1 %all-to-all-start.2 = ((f32[128,64,128]{2,1,0:T(8,128)}), f32[128,64,128]{2,1,0:T(8,128)}, u32[]{:S(2)}, u32[]{:S(2)}) async-start(f32[128,64,128]{2,1,0:T(8,128)} %asked.2), calls=%async_computation.2 | async-start | bytes 8388608 | tf_op jit(solution)/shard_map/all_to_all | solution.py:402
  91.1 0.8 copy.46.cores
  91.8 20.0 %item_side.1 = (bf16[128,64,128]{2,1,0:T(8,128)(2,1)}, f32[128,64,128]{2,1,0:T(8,128)}, bf16[512,128,128]{2,1,0:T(8,128)(2,1)}, bf16[128,128,128]{2,1,0:T(8,128)(2,1)}) custom-call(s32[512]{0:T(512)} %slots_user.3, s32[512]{0:T(512)} %slots_item.3, s32[512]{0:T(512)} %steps.3, s32[1]{0:T(128)S(6)} %copy.57.count, f32[128,64,128]{2,1,0:T(8,128)} %all-to-all-done.1.items, ...), custom_call_target="tpu_custom_call" | custom-call | flops 20000000000 | bytes 50000000 | tf_op jit(solution)/shard_map/item_side/pallas_call | solution.py:121
  111.8 31.1 %all-to-all-done.2.users = f32[128,64,128]{2,1,0:T(8,128)} async-done(((f32[128,64,128]{2,1,0:T(8,128)}), f32[128,64,128]{2,1,0:T(8,128)}, u32[]{:S(2)}, u32[]{:S(2)}) %all-to-all-start.2) | async-done | bytes 4194336 | tf_op jit(solution)/shard_map/all_to_all | solution.py:402
  143.0 6.3 %user_grad.1 = f32[128,64,128]{2,1,0:T(8,128)} custom-call(f32[128,64,128]{2,1,0:T(8,128)} %all-to-all-done.2.users, bf16[128,64,128]{2,1,0:T(8,128)(2,1)} %get-tuple-element.39.gram, f32[128,64,128]{2,1,0:T(8,128)} %get-tuple-element.40.moved), custom_call_target="tpu_custom_call" | custom-call | flops 1000000000 | bytes 20000000 | tf_op jit(solution)/shard_map/user_grad/pallas_call | solution.py:176
  149.3 6.1 %all-to-all-start.3 = ((f32[128,64,128]{2,1,0:T(8,128)}), f32[128,64,128]{2,1,0:T(8,128)}, u32[]{:S(2)}, u32[]{:S(2)}) async-start(f32[128,64,128]{2,1,0:T(8,128)} %user_grad.1), calls=%async_computation.3 | async-start | bytes 8388608 | tf_op jit(solution)/shard_map/all_to_all | solution.py:402
  155.4 22.5 %tile_side.1 = (f32[128,72,128]{2,1,0:T(8,128)}, f32[8,64,64]{2,1,0:T(8,128)}) custom-call(s32[512]{0:T(512)} %slots_user.3, s32[512]{0:T(512)} %slots_item.3, s32[512]{0:T(512)} %steps.3, s32[1]{0:T(128)S(6)} %copy.57.count, f32[128,64,128]{2,1,0:T(8,128)} %all-to-all-done.2.users, bf16[128,128,128]{2,1,0:T(8,128)(2,1)} %get-tuple-element.42.right, ...), custom_call_target="tpu_custom_call" | custom-call | flops 30000001024 | bytes 50000000 | tf_op jit(solution)/shard_map/tile_side/pallas_call | solution.py:244
  177.8 1.1 reshape.68
  179.2 28.6 %all-to-all-done.3.back = f32[128,64,128]{2,1,0:T(8,128)} async-done(((f32[128,64,128]{2,1,0:T(8,128)}), f32[128,64,128]{2,1,0:T(8,128)}, u32[]{:S(2)}, u32[]{:S(2)}) %all-to-all-start.3) | async-done | bytes 4194336 | tf_op jit(solution)/shard_map/all_to_all | solution.py:402
  208.0 16.3 %all_to_all.38 = f32[128,4,128]{2,1,0:T(4,128)S(1)} all-to-all(f32[128,4,128]{2,1,0:T(4,128)S(1)} %copy.49), channel_id=1, replica_groups=mesh['tm'=16,'rows'=8] {'tm','rows'}, dimensions={0} | all-to-all | bytes 524288 | tf_op jit(solution)/shard_map/all_to_all | solution.py:402
  225.1 0.9 constant_dynamic-update-slice_fusion
  226.0 5.4 %all-to-all-start.5 = ((f32[128,72,128]{2,1,0:T(8,128)}), f32[128,72,128]{2,1,0:T(8,128)}, u32[]{:S(2)}, u32[]{:S(2)}) async-start(f32[128,72,128]{2,1,0:T(8,128)} %constant_dynamic-update-slice_fusion), calls=%async_computation.5 | async-start | bytes 9437184 | tf_op jit(solution)/shard_map/all_to_all | solution.py:402
  231.5 3.8 %owner_sum.1 = f32[8,64,128]{2,1,0:T(8,128)} custom-call(s32[128]{0:T(128)} %get-tuple-element.57.held, f32[128,64,128]{2,1,0:T(8,128)} %all-to-all-done.3.back), custom_call_target="tpu_custom_call" | custom-call | flops 10000000 | bytes 10000000 | tf_op jit(solution)/shard_map/owner_sum/pallas_call | solution.py:325
  235.3 1.2 convolution_bitcast_fusion
  236.6 1.4 collective-permute-start
  237.9 0.8 collective-permute-done
  239.3 45.0 %collective-permute-done.1 = f32[8,64]{1,0:T(8,128)S(1)} collective-permute-done((f32[8,64]{1,0:T(8,128)S(1)}, f32[8,64]{1,0:T(8,128)S(1)}, u32[]{:S(2)}, u32[]{:S(2)}) %collective-permute-start.1) | collective-permute-done | bytes 2080 | tf_op jit(solution)/shard_map/ppermute | solution.py:407
  284.3 2.9 collective-permute-start.2
  287.2 1.5 collective-permute-done.2
  289.3 0.9 all-to-all-done.5.back
  290.2 1.1 slice.41.mine
  291.2 1.2 collective-permute-start.3
  292.4 1.5 collective-permute-done.3.other
  294.0 4.6 %owner_core_sum.1 = (f32[8,64,128]{2,1,0:T(8,128)}, f32[128,32,64]{2,1,0:T(8,128)}) custom-call(s32[128]{0:T(128)S(1)} %copy-done.1, s32[1]{0:T(128)} %bitcast.11.odd, f32[128,72,128]{2,1,0:T(8,128)} %all-to-all-done.5.back, f32[128,8,128]{2,1,0:T(8,128)S(1)} %slice.41.mine, f32[128,8,128]{2,1,0:T(8,128)S(1)} %collective-permute-done.3.other), custom_call_target="tpu_custom_call" | custom-call | flops 10000000 | bytes 10000000 | tf_op jit(solution)/shard_map/owner_core_sum/pallas_call | solution.py:380
  (27 shorter events, 2.5 us)
Async XLA Ops:
  0.6 31.0 %copy-start = (f32[64,64,64]{2,1,0:T(8,128)S(1)}, f32[64,64,64]{2,1,0:T(8,128)}, u32[]{:S(2)}) copy-start(f32[64,64,64]{2,1,0:T(8,128)} %param.23) | copy-start | bytes 3145732
  26.1 5.5 %copy-start.3 = (f32[8,64]{1,0:T(8,128)S(1)}, f32[8,64]{1,0:T(8,128)}, u32[]{:S(2)}) copy-start(f32[8,64]{1,0:T(8,128)} %param.22) | copy-start | bytes 6148
  26.2 58.1 %all-to-all-start.1 = ((f32[128,64,128]{2,1,0:T(8,128)}), f32[128,64,128]{2,1,0:T(8,128)}, u32[]{:S(2)}, u32[]{:S(2)}) async-start(f32[128,64,128]{2,1,0:T(8,128)} %asked.3), calls=%async_computation.1 | async-start | bytes 8388608 | tf_op jit(solution)/shard_map/all_to_all | solution.py:402
  84.3 58.7 %all-to-all-start.2 = ((f32[128,64,128]{2,1,0:T(8,128)}), f32[128,64,128]{2,1,0:T(8,128)}, u32[]{:S(2)}, u32[]{:S(2)}) async-start(f32[128,64,128]{2,1,0:T(8,128)} %asked.2), calls=%async_computation.2 | async-start | bytes 8388608 | tf_op jit(solution)/shard_map/all_to_all | solution.py:402
  149.3 58.6 %all-to-all-start.3 = ((f32[128,64,128]{2,1,0:T(8,128)}), f32[128,64,128]{2,1,0:T(8,128)}, u32[]{:S(2)}, u32[]{:S(2)}) async-start(f32[128,64,128]{2,1,0:T(8,128)} %user_grad.1), calls=%async_computation.3 | async-start | bytes 8388608 | tf_op jit(solution)/shard_map/all_to_all | solution.py:402
  226.0 64.1 %all-to-all-start.5 = ((f32[128,72,128]{2,1,0:T(8,128)}), f32[128,72,128]{2,1,0:T(8,128)}, u32[]{:S(2)}, u32[]{:S(2)}) async-start(f32[128,72,128]{2,1,0:T(8,128)} %constant_dynamic-update-slice_fusion), calls=%async_computation.5 | async-start | bytes 9437184 | tf_op jit(solution)/shard_map/all_to_all | solution.py:402
  231.5 3.9 %copy-start.2 = (f32[8,64,64]{2,1,0:T(8,128)S(1)}, f32[8,64,64]{2,1,0:T(8,128)}, u32[]{:S(2)}) copy-start(f32[8,64,64]{2,1,0:T(8,128)} %get-tuple-element.50) | copy-start | bytes 393220
  231.5 62.5 %copy-start.1 = (s32[128]{0:T(128)S(1)}, s32[128]{0:T(128)}, u32[]{:S(2)}) copy-start(s32[128]{0:T(128)} %get-tuple-element.56.held) | copy-start | bytes 1540
  236.6 2.2 collective-permute-start
  238.7 45.6 %collective-permute-start.1 = (f32[8,64]{1,0:T(8,128)S(1)}, f32[8,64]{1,0:T(8,128)S(1)}, u32[]{:S(2)}, u32[]{:S(2)}) collective-permute-start(f32[8,64]{1,0:T(8,128)S(1)} %add.23), channel_id=1, source_target_pairs={{0,2},{1,3},{2,0},{3,1},{4,6},{5,7},{6,4},{7,5},{8,10},{9,11},{10,... | collective-permute-start | bytes 6152 | tf_op jit(solution)/shard_map/ppermute | solution.py:407
  284.3 4.4 %collective-permute-start.2 = (f32[8,64]{1,0:T(8,128)S(1)}, f32[8,64]{1,0:T(8,128)S(1)}, u32[]{:S(2)}, u32[]{:S(2)}) collective-permute-start(f32[8,64]{1,0:T(8,128)S(1)} %add.24), channel_id=1, source_target_pairs={{0,4},{1,5},{2,6},{3,7},{4,0},{5,1},{6,2},{7,3},{8,12},{9,13},{10,... | collective-permute-start | bytes 6152 | tf_op jit(solution)/shard_map/ppermute | solution.py:407
  291.2 2.7 collective-permute-start.3
